TPU v7x, 32 devices: a whole 2x2x4 slice. The times are simulated.
32 devices in a mesh: phase: 4 (over y, x), batch: 8 (over z, core).
Axes of the slice: x: 2, y: 2, z: 4, core: 2. Of those that a mesh axis runs over, the one named last changes fastest.
Arguments:
- features: bfloat16 [256000, 256], P('batch'), may hold values from -6 to 6
- weights: bfloat16 [4, 213504], P('phase')
- crop_kind: int32 [8, 4, 5], replicated, may hold values from 0 to 3, as said below
- positives: int32 [8, 4, 5], P('batch'), may hold values from 0 to 16383
- negatives: int32 [8, 4, 5, 4096], P('batch'), may hold values from 0 to 16383
- bank: float32 [16384, 128], replicated, may hold values from -0.5 to 0.5
- normalizer: float32 [1], replicated, may hold values from 1024 to 262144
Outputs:
- weight_grads: float32 [4, 213504], P('phase')
- input_grad: bfloat16 [256000, 256], P(('batch', 'phase'))
Inputs may be any that keep to these rules, and one draw needn't show every extreme that they name: `crop_kind`: 0 is an empty slot, 1, 2, 3 the crop classes; live slots come first; the input pixels of one device's micro-batch sum to at most 8000, and in every draw one device's micro-batch holds five class-1 crops filling 8000 exactly.
All inputs are finite; a program needn't handle non-finite values.
Results may differ from a plain program's by a relative error of at most 0.017.
Values may be sent and summed in bfloat16 or wider, within the bound.
A program may use at most 320 MiB of HBM per device.

v0:
```python
import jax
import jax.numpy as jnp
from jax import lax
from jax.sharding import PartitionSpec as P

CIN = 256
MID = 128
COUT = 512
EMB = 128
SIDE_UNIT = 4
MICRO = 4
NEG = 4096
BANK = 16384
GRAD_LEN = 213504


SOFTMAX_TEMPER = 0.07
EPSILON = 1e-05
HIGHEST_PRECISE = lax.Precision.HIGHEST


def as_sent(value):

    def short(part):
        return part.astype(jnp.bfloat16) if part.dtype == jnp.float32 else part

    return jax.tree.map(short, value)


def shifted(block, axis, distance):
    devices = range(lax.axis_size(axis))
    route = [(i - distance, i) for i in devices if i - distance in devices]
    return lax.ppermute(block, axis, route)


def layout(section):
    if section == 0:
        return (
            ("conv_in", (CIN, MID), 0),
            ("gain_in", (MID,), 1),
            ("bias_in", (MID,), 2),
            ("conv_mid", (9 * MID, MID), 0),
            ("gain_mid", (MID,), 1),
            ("bias_mid", (MID,), 2),
        )
    if section == 1:
        return (
            ("conv_out", (MID, COUT), 0),
            ("gain_out", (COUT,), 1),
            ("bias_out", (COUT,), 2),
            ("shortcut", (CIN, COUT), 0),
            ("gain_short", (COUT,), 1),
            ("bias_short", (COUT,), 2),
        )
    if section == 2:
        return (
            ("conv_in", (COUT, MID), 0),
            ("gain_in", (MID,), 1),
            ("bias_in", (MID,), 2),
            ("conv_mid", (9 * MID, MID), 0),
            ("gain_mid", (MID,), 1),
            ("bias_mid", (MID,), 2),
        )
    return (
        ("conv_out", (MID, COUT), 0),
        ("gain_out", (COUT,), 1),
        ("bias_out", (COUT,), 2),
        ("head", (COUT, EMB), 0),
    )


def entry_count(shape):
    count = 1
    for extent in shape:
        count = count * extent
    return count


def unpack(flat, section):
    pieces = {}
    offset = 0
    for name, shape, kind in layout(section):
        count = entry_count(shape)
        pieces[name] = flat[offset : offset + count].reshape(shape)
        offset = offset + count
    return pieces


def pack_some(section, gradients):
    parts_list = []
    for name, shape, kind in layout(section):
        if name in gradients:
            parts_list.append(gradients[name].reshape(-1))
        else:
            parts_list.append(jnp.zeros((entry_count(shape),), jnp.float32))
    vector = jnp.concatenate(parts_list)
    return jnp.pad(vector, (0, GRAD_LEN - vector.shape[0]))


def side_lengths(kinds):
    return (
        SIDE_UNIT * jnp.where(kinds == 1, 5, jnp.where(kinds == 2, 7, jnp.where(kinds == 3, 9, 0)))
    ).astype(jnp.int32)


def geometry(kinds, out_rows):
    sides = side_lengths(kinds)
    areas = sides * sides
    starts = jnp.cumsum(areas, dtype=jnp.int32) - areas
    rows = jnp.arange(out_rows, dtype=jnp.int32)
    inside = (
        (rows[:, None] >= starts[None, :]) & (rows[:, None] < (starts + areas)[None, :])
    ).astype(jnp.int32)
    live = jnp.sum(inside, axis=1, dtype=jnp.int32) > 0
    width = jnp.maximum(jnp.sum(inside * sides[None, :], axis=1, dtype=jnp.int32), 1)
    local = rows - jnp.sum(inside * starts[None, :], axis=1, dtype=jnp.int32)
    base = rows - local
    return (inside, live, width, local // width, local % width, base)


def taps(width, row_pos, col_pos, base, live, stride):
    full = stride * width
    index_list = []
    valid_list = []
    for shift_row in range(3):
        for shift_col in range(3):
            pos_row = stride * row_pos + shift_row - 1
            pos_col = stride * col_pos + shift_col - 1
            valid = live & (pos_row >= 0) & (pos_row < full) & (pos_col >= 0) & (pos_col < full)
            index_list.append(
                jnp.where(valid, stride * stride * base + pos_row * full + pos_col, 0)
            )
            valid_list.append(valid)
    return (jnp.stack(index_list, axis=1), jnp.stack(valid_list, axis=1))


def gather_taps(source, index, valid):
    picked = jnp.take(source, index.reshape(-1), axis=0).reshape(index.shape[0], 9, source.shape[1])
    picked = picked * valid[:, :, None].astype(source.dtype)
    return picked.reshape(index.shape[0], 9 * source.shape[1])


def scatter_taps(columns, index, valid, total_rows, channels):
    spread = columns.reshape(index.shape[0], 9, channels) * valid[:, :, None].astype(jnp.float32)
    return jax.ops.segment_sum(
        spread.reshape(-1, channels), index.reshape(-1), num_segments=total_rows
    )


def dense(left, right):
    return jnp.dot(left, right, preferred_element_type=jnp.float32)


def outer(left, right):
    return jnp.einsum("rc,rd->cd", left, right, preferred_element_type=jnp.float32)


def silu_slope(values):
    sigma = jax.nn.sigmoid(values)
    return sigma * (1.0 + values * (1.0 - sigma))


def norm_local(values, live):
    mask = live.astype(jnp.float32)[:, None]
    return jnp.stack([jnp.sum(values * mask, axis=0), jnp.sum(values * values * mask, axis=0)])


def pad_pair(local):
    return jnp.pad(local, ((0, 0), (0, 2 * COUT - local.shape[1])))


def norm_totals(local):
    return lax.psum(local, "batch")


def norm_back_totals(local):
    return lax.psum(local, "batch")


def finish_stats(totals, count):
    mean = totals[0] / count
    inverse = lax.rsqrt(totals[1] / count - mean * mean + EPSILON)
    return (mean, inverse)


def norm_back_local(upstream, unit_features, live, gain):
    mask = live.astype(jnp.float32)[:, None]
    scaled = upstream * gain * mask
    local = jnp.stack([jnp.sum(scaled, axis=0), jnp.sum(scaled * unit_features, axis=0)])
    gain_grad = jnp.sum(upstream * unit_features * mask, axis=0)
    bias_grad = jnp.sum(upstream * mask, axis=0)
    return (scaled, local, gain_grad, bias_grad)


def norm_back_finish(scaled, unit_features, totals, inverse, count, live):
    mask = live.astype(jnp.float32)[:, None]
    return mask * inverse * (scaled - totals[0] / count - unit_features * totals[1] / count)


def replace(state, position, value):
    items = list(state)
    items[position] = value
    return tuple(items)


def shards(features, weights, crop_kind, positives, negatives, bank, normalizer):
    phase = lax.axis_index("phase")
    phases = lax.axis_size("phase")
    batch_index = lax.axis_index("batch")
    channels = features.shape[1]
    in_rows = features.shape[0] // MICRO
    out_rows = in_rows // 4
    wide = MID + max(CIN, COUT)
    inputs = features.reshape(MICRO, in_rows, channels)
    params = [unpack(weights[0], section) for section in range(4)]
    float_params = [
        {name: value.astype(jnp.float32) for name, value in group.items()} for group in params
    ]
    all_sides = side_lengths(crop_kind).astype(jnp.float32)
    out_counts = jnp.sum(all_sides * all_sides, axis=(0, 2))
    mine = lax.dynamic_index_in_dim(crop_kind, batch_index, 0, keepdims=False)
    own_positive = positives[0]
    own_negative = negatives[0]
    log_offset = jnp.log(normalizer[0] * NEG / BANK)
    zero_local = jnp.zeros((2, 2 * COUT), jnp.float32)

    def micro_geometry(micro):
        kinds = lax.dynamic_index_in_dim(mine, micro, 0, keepdims=False)
        inside, live, width, row_pos, col_pos, base = geometry(kinds, out_rows)
        sides = side_lengths(kinds)
        live_in = jnp.arange(in_rows, dtype=jnp.int32) < 4 * jnp.sum(sides * sides, dtype=jnp.int32)
        wide_index, wide_valid = taps(width, row_pos, col_pos, base, live, 2)
        near_index, near_valid = taps(width, row_pos, col_pos, base, live, 1)
        sub_index = jnp.where(live, 4 * base + 4 * row_pos * width + 2 * col_pos, 0)
        areas = (sides * sides).astype(jnp.float32)
        return (
            inside,
            live,
            live_in,
            wide_index,
            wide_valid,
            near_index,
            near_valid,
            sub_index,
            areas,
            kinds,
        )

    def pad_columns(parts_list):
        used = sum((piece.shape[1] for piece in parts_list))
        return jnp.concatenate(
            parts_list + [jnp.zeros((out_rows, wide - used), jnp.bfloat16)], axis=1
        )

    def micro_input(micro):
        return lax.dynamic_index_in_dim(inputs, micro, 0, keepdims=False)

    def put_stats(stats, row, vector):
        return stats.at[row, : vector.shape[0]].set(vector)

    def first_open(received, micro, state, totals):
        info = micro_geometry(micro)
        conv_first = dense(micro_input(micro), params[0]["conv_in"])
        return (replace(state, 0, conv_first), pad_pair(norm_local(conv_first, info[2])))

    def first_middle(received, micro, state, totals):
        info = micro_geometry(micro)
        gains = float_params[0]
        mean_one, inverse_one = finish_stats(totals[:, :MID], 4.0 * out_counts[micro])
        hidden_one = jax.nn.silu(
            (state[0] - mean_one) * inverse_one * gains["gain_in"] + gains["bias_in"]
        ).astype(jnp.bfloat16)
        columns = gather_taps(hidden_one, info[3], info[4])
        conv_second = dense(columns, params[0]["conv_mid"])
        stats = put_stats(put_stats(state[5], 0, mean_one), 1, inverse_one)
        state = replace(replace(state, 1, conv_second), 5, stats)
        return (state, pad_pair(norm_local(conv_second, info[1])))

    def first_close(received, micro, state, totals):
        gains = float_params[0]
        mean_two, inverse_two = finish_stats(totals[:, :MID], out_counts[micro])
        hidden_two = jax.nn.silu(
            (state[1] - mean_two) * inverse_two * gains["gain_mid"] + gains["bias_mid"]
        ).astype(jnp.bfloat16)
        stats = put_stats(put_stats(state[5], 2, mean_two), 3, inverse_two)
        return (replace(replace(state, 4, pad_columns([hidden_two])), 5, stats), zero_local)

    def second_open(received, micro, state, totals):
        info = micro_geometry(micro)
        live = info[1]
        conv_third = dense(received[:, :MID], params[1]["conv_out"])
        picked = jnp.take(micro_input(micro), info[7], axis=0) * live[:, None].astype(jnp.bfloat16)
        conv_short = dense(picked, params[1]["shortcut"])
        local = jnp.concatenate(
            [norm_local(conv_third, live), norm_local(conv_short, live)], axis=1
        )
        return (replace(replace(state, 2, conv_third), 3, conv_short), local)

    def second_middle(received, micro, state, totals):
        gains = float_params[1]
        count = out_counts[micro]
        mean_out, inverse_out = finish_stats(totals[:, :COUT], count)
        mean_short, inverse_short = finish_stats(totals[:, COUT:], count)
        branch = (state[2] - mean_out) * inverse_out * gains["gain_out"] + gains["bias_out"]
        short = (state[3] - mean_short) * inverse_short * gains["gain_short"] + gains["bias_short"]
        block = jax.nn.silu(branch + short).astype(jnp.bfloat16)
        stats = jnp.stack([mean_out, inverse_out, mean_short, inverse_short])
        return (replace(replace(state, 4, pad_columns([block])), 5, stats), zero_local)

    def pass_through(received, micro, state, totals):
        return (state, zero_local)

    def third_open(received, micro, state, totals):
        info = micro_geometry(micro)
        conv_fourth = dense(received[:, :COUT], params[2]["conv_in"])
        return (replace(state, 1, conv_fourth), pad_pair(norm_local(conv_fourth, info[1])))

    def third_middle(received, micro, state, totals):
        info = micro_geometry(micro)
        gains = float_params[2]
        mean_one, inverse_one = finish_stats(totals[:, :MID], out_counts[micro])
        hidden_three = jax.nn.silu(
            (state[1] - mean_one) * inverse_one * gains["gain_in"] + gains["bias_in"]
        ).astype(jnp.bfloat16)
        columns = gather_taps(hidden_three, info[5], info[6])
        conv_fifth = dense(columns, params[2]["conv_mid"])
        stats = put_stats(put_stats(state[5], 0, mean_one), 1, inverse_one)
        state = replace(replace(state, 1, conv_fifth), 5, stats)
        return (state, pad_pair(norm_local(conv_fifth, info[1])))

    def third_close(received, micro, state, totals):
        gains = float_params[2]
        mean_two, inverse_two = finish_stats(totals[:, :MID], out_counts[micro])
        hidden_four = jax.nn.silu(
            (state[1] - mean_two) * inverse_two * gains["gain_mid"] + gains["bias_mid"]
        ).astype(jnp.bfloat16)
        stats = put_stats(put_stats(state[5], 2, mean_two), 3, inverse_two)
        leaving = pad_columns([hidden_four, received[:, :COUT]])
        return (replace(replace(state, 4, leaving), 5, stats), zero_local)

    def fourth_open(received, micro, state, totals):
        info = micro_geometry(micro)
        conv_sixth = dense(received[:, :MID], params[3]["conv_out"])
        return (replace(state, 2, conv_sixth), pad_pair(norm_local(conv_sixth, info[1])))

    def fourth_middle(received, micro, state, totals):
        mean_out, inverse_out = finish_stats(totals[:, :COUT], out_counts[micro])
        stats = put_stats(put_stats(state[5], 0, mean_out), 1, inverse_out)
        return (replace(state, 5, stats), zero_local)

    forward_open = [first_open, second_open, third_open, fourth_open]
    forward_middle = [first_middle, second_middle, third_middle, fourth_middle]
    forward_close = [first_close, pass_through, third_close, pass_through]

    def forward_blank():
        return (
            jnp.zeros((in_rows, MID), jnp.float32),
            jnp.zeros((out_rows, MID), jnp.float32),
            jnp.zeros((out_rows, COUT), jnp.float32),
            jnp.zeros((out_rows, COUT), jnp.float32),
            jnp.zeros((out_rows, wide), jnp.bfloat16),
            jnp.zeros((4, COUT), jnp.float32),
        )

    def back_first_open(received, kept, stats, micro, state, totals):
        info = micro_geometry(micro)
        live, live_in = (info[1], info[2])
        pieces, gains = (params[0], float_params[0])
        conv_first = dense(micro_input(micro), pieces["conv_in"])
        normed_one = (conv_first - stats[0, :MID]) * stats[1, :MID]
        hidden_one = jax.nn.silu(normed_one * gains["gain_in"] + gains["bias_in"]).astype(
            jnp.bfloat16
        )
        columns = gather_taps(hidden_one, info[3], info[4])
        conv_second = dense(columns, pieces["conv_mid"])
        normed_two = (conv_second - stats[2, :MID]) * stats[3, :MID]
        pre_two = normed_two * gains["gain_mid"] + gains["bias_mid"]
        pre_two_grad = received[:, :MID].astype(jnp.float32) * silu_slope(pre_two)
        scaled_two, local_two, gain_mid_grad, bias_mid_grad = norm_back_local(
            pre_two_grad, normed_two, live, gains["gain_mid"]
        )
        state = replace(replace(replace(state, 0, normed_one), 2, scaled_two), 3, normed_two)
        state = replace(
            state, 10, pack_some(0, {"gain_mid": gain_mid_grad, "bias_mid": bias_mid_grad})
        )
        return (state, pad_pair(local_two))

    def back_first_middle(received, kept, stats, micro, state, totals):
        info = micro_geometry(micro)
        live, live_in = (info[1], info[2])
        count = out_counts[micro]
        pieces, gains = (params[0], float_params[0])
        second_grad = norm_back_finish(
            state[2], state[3], totals[:, :MID], stats[3, :MID], count, live
        ).astype(jnp.bfloat16)
        normed_one = state[0]
        pre_one = normed_one * gains["gain_in"] + gains["bias_in"]
        hidden_one = jax.nn.silu(pre_one).astype(jnp.bfloat16)
        columns = gather_taps(hidden_one, info[3], info[4])
        mid_grad = outer(columns, second_grad)
        hidden_one_grad = scatter_taps(
            dense(second_grad, pieces["conv_mid"].T), info[3], info[4], in_rows, MID
        )
        pre_one_grad = hidden_one_grad * silu_slope(pre_one)
        scaled_one, local_one, gain_in_grad, bias_in_grad = norm_back_local(
            pre_one_grad, normed_one, live_in, gains["gain_in"]
        )
        grad_vec = state[10] + pack_some(
            0, {"conv_mid": mid_grad, "gain_in": gain_in_grad, "bias_in": bias_in_grad}
        )
        return (replace(replace(state, 1, scaled_one), 10, grad_vec), pad_pair(local_one))

    def back_first_close(received, kept, stats, micro, state, totals):
        info = micro_geometry(micro)
        live, live_in, sub_index = (info[1], info[2], info[7])
        count = out_counts[micro]
        pieces = params[0]
        source = micro_input(micro)
        first_grad = norm_back_finish(
            state[1], state[0], totals[:, :MID], stats[1, :MID], 4.0 * count, live_in
        ).astype(jnp.bfloat16)
        in_grad = outer(source, first_grad)
        short_rows = received[:, MID : MID + CIN].astype(jnp.float32) * live[:, None].astype(
            jnp.float32
        )
        source_grad = dense(first_grad, pieces["conv_in"].T) + jax.ops.segment_sum(
            short_rows, sub_index, num_segments=in_rows
        )
        grad_vec = state[10] + pack_some(0, {"conv_in": in_grad})
        return (replace(replace(state, 10, grad_vec), 11, source_grad), zero_local)

    def second_recompute(kept, stats, micro):
        info = micro_geometry(micro)
        live = info[1]
        pieces = params[1]
        hidden_two = kept[:, :MID]
        conv_third = dense(hidden_two, pieces["conv_out"])
        normed_out = (conv_third - stats[0]) * stats[1]
        picked = jnp.take(micro_input(micro), info[7], axis=0) * live[:, None].astype(jnp.bfloat16)
        conv_short = dense(picked, pieces["shortcut"])
        normed_short = (conv_short - stats[2]) * stats[3]
        return (live, hidden_two, picked, normed_out, normed_short)

    def back_second_open(received, kept, stats, micro, state, totals):
        gains = float_params[1]
        live, hidden_two, picked, normed_out, normed_short = second_recompute(kept, stats, micro)
        pre = (
            normed_out * gains["gain_out"]
            + gains["bias_out"]
            + (normed_short * gains["gain_short"] + gains["bias_short"])
        )
        pre_grad = received[:, :COUT].astype(jnp.float32) * silu_slope(pre)
        scaled_out, local_out, gain_out_grad, bias_out_grad = norm_back_local(
            pre_grad, normed_out, live, gains["gain_out"]
        )
        scaled_short, local_short, gain_short_grad, bias_short_grad = norm_back_local(
            pre_grad, normed_short, live, gains["gain_short"]
        )
        state = replace(
            replace(replace(replace(state, 5, scaled_out), 6, normed_out), 7, scaled_short),
            8,
            normed_short,
        )
        grad_vec = pack_some(
            1,
            {
                "gain_out": gain_out_grad,
                "bias_out": bias_out_grad,
                "gain_short": gain_short_grad,
                "bias_short": bias_short_grad,
            },
        )
        return (replace(state, 10, grad_vec), jnp.concatenate([local_out, local_short], axis=1))

    def back_second_middle(received, kept, stats, micro, state, totals):
        info = micro_geometry(micro)
        live = info[1]
        count = out_counts[micro]
        pieces = params[1]
        hidden_two = kept[:, :MID]
        picked = jnp.take(micro_input(micro), info[7], axis=0) * live[:, None].astype(jnp.bfloat16)
        third_grad = norm_back_finish(
            state[5], state[6], totals[:, :COUT], stats[1], count, live
        ).astype(jnp.bfloat16)
        short_grad = norm_back_finish(
            state[7], state[8], totals[:, COUT:], stats[3], count, live
        ).astype(jnp.bfloat16)
        hidden_two_grad = dense(third_grad, pieces["conv_out"].T).astype(jnp.bfloat16)
        picked_grad = dense(short_grad, pieces["shortcut"].T).astype(jnp.bfloat16)
        grad_vec = state[10] + pack_some(
            1, {"conv_out": outer(hidden_two, third_grad), "shortcut": outer(picked, short_grad)}
        )
        return (
            replace(replace(state, 9, pad_columns([hidden_two_grad, picked_grad])), 10, grad_vec),
            zero_local,
        )

    def back_pass(received, kept, stats, micro, state, totals):
        return (state, zero_local)

    def back_third_open(received, kept, stats, micro, state, totals):
        info = micro_geometry(micro)
        live = info[1]
        pieces, gains = (params[2], float_params[2])
        block = kept[:, :COUT]
        conv_fourth = dense(block, pieces["conv_in"])
        normed_one = (conv_fourth - stats[0, :MID]) * stats[1, :MID]
        hidden_three = jax.nn.silu(normed_one * gains["gain_in"] + gains["bias_in"]).astype(
            jnp.bfloat16
        )
        columns = gather_taps(hidden_three, info[5], info[6])
        conv_fifth = dense(columns, pieces["conv_mid"])
        normed_two = (conv_fifth - stats[2, :MID]) * stats[3, :MID]
        pre_two = normed_two * gains["gain_mid"] + gains["bias_mid"]
        pre_two_grad = received[:, :MID].astype(jnp.float32) * silu_slope(pre_two)
        scaled_two, local_two, gain_mid_grad, bias_mid_grad = norm_back_local(
            pre_two_grad, normed_two, live, gains["gain_mid"]
        )
        state = replace(replace(replace(state, 2, scaled_two), 3, normed_two), 4, normed_one)
        state = replace(
            state, 10, pack_some(2, {"gain_mid": gain_mid_grad, "bias_mid": bias_mid_grad})
        )
        return (state, pad_pair(local_two))

    def back_third_middle(received, kept, stats, micro, state, totals):
        info = micro_geometry(micro)
        live = info[1]
        count = out_counts[micro]
        pieces, gains = (params[2], float_params[2])
        fifth_grad = norm_back_finish(
            state[2], state[3], totals[:, :MID], stats[3, :MID], count, live
        ).astype(jnp.bfloat16)
        normed_one = state[4]
        pre_one = normed_one * gains["gain_in"] + gains["bias_in"]
        hidden_three = jax.nn.silu(pre_one).astype(jnp.bfloat16)
        columns = gather_taps(hidden_three, info[5], info[6])
        mid_grad = outer(columns, fifth_grad)
        hidden_three_grad = scatter_taps(
            dense(fifth_grad, pieces["conv_mid"].T), info[5], info[6], out_rows, MID
        )
        pre_one_grad = hidden_three_grad * silu_slope(pre_one)
        scaled_one, local_one, gain_in_grad, bias_in_grad = norm_back_local(
            pre_one_grad, normed_one, live, gains["gain_in"]
        )
        grad_vec = state[10] + pack_some(
            2, {"conv_mid": mid_grad, "gain_in": gain_in_grad, "bias_in": bias_in_grad}
        )
        return (replace(replace(state, 2, scaled_one), 10, grad_vec), pad_pair(local_one))

    def back_third_close(received, kept, stats, micro, state, totals):
        info = micro_geometry(micro)
        live = info[1]
        count = out_counts[micro]
        pieces = params[2]
        block = kept[:, :COUT]
        fourth_grad = norm_back_finish(
            state[2], state[4], totals[:, :MID], stats[1, :MID], count, live
        ).astype(jnp.bfloat16)
        block_grad = (
            dense(fourth_grad, pieces["conv_in"].T)
            + received[:, MID : MID + COUT].astype(jnp.float32)
        ).astype(jnp.bfloat16)
        grad_vec = state[10] + pack_some(2, {"conv_in": outer(block, fourth_grad)})
        return (replace(replace(state, 9, pad_columns([block_grad])), 10, grad_vec), zero_local)

    def back_fourth_open(received, kept, stats, micro, state, totals):
        info = micro_geometry(micro)
        inside, live, areas, kinds = (info[0], info[1], info[8], info[9])
        pieces, gains = (params[3], float_params[3])
        hidden_four = kept[:, :MID]
        carried = kept[:, MID : MID + COUT].astype(jnp.float32)
        conv_sixth = dense(hidden_four, pieces["conv_out"])
        normed_out = (conv_sixth - stats[0]) * stats[1]
        pre = normed_out * gains["gain_out"] + gains["bias_out"] + carried
        final = jax.nn.silu(pre)
        share = inside.astype(jnp.float32) / jnp.maximum(areas, 1.0)[None, :]
        pooled = jnp.einsum("rs,rc->sc", share, final, precision=HIGHEST_PRECISE)
        head = gains["head"]
        embed = jnp.dot(pooled, head, precision=HIGHEST_PRECISE)
        scale = lax.rsqrt(jnp.sum(embed * embed, axis=-1, keepdims=True) + 1e-06)
        unit_features = embed * scale
        logit_scores = jnp.dot(unit_features, bank.T, precision=HIGHEST_PRECISE) / SOFTMAX_TEMPER
        pos_ids = lax.dynamic_index_in_dim(own_positive, micro, 0, keepdims=False)
        neg_ids = lax.dynamic_index_in_dim(own_negative, micro, 0, keepdims=False)
        positive = jnp.take_along_axis(logit_scores, pos_ids[:, None], axis=1)[:, 0]
        negative = jnp.take_along_axis(logit_scores, neg_ids, axis=1)
        present = (kinds > 0).astype(jnp.float32)
        positive_grad = -jax.nn.sigmoid(log_offset - positive) * present
        negative_grad = jax.nn.sigmoid(negative - log_offset) * present[:, None]
        slot_rows = jnp.arange(kinds.shape[0], dtype=jnp.int32)
        logit_score_grad = (
            jnp.zeros(logit_scores.shape, jnp.float32)
            .at[slot_rows[:, None], neg_ids]
            .add(negative_grad)
        )
        logit_score_grad = logit_score_grad.at[slot_rows, pos_ids].add(positive_grad)
        unit_features_grad = (
            jnp.dot(logit_score_grad, bank, precision=HIGHEST_PRECISE) / SOFTMAX_TEMPER
        )
        embed_grad = scale * unit_features_grad - embed * scale * scale * scale * jnp.sum(
            embed * unit_features_grad, axis=-1, keepdims=True
        )
        head_grad = jnp.einsum("sc,se->ce", pooled, embed_grad, precision=HIGHEST_PRECISE)
        pooled_grad = jnp.dot(embed_grad, head.T, precision=HIGHEST_PRECISE)
        final_grad = jnp.dot(share, pooled_grad, precision=HIGHEST_PRECISE)
        pre_grad = final_grad * silu_slope(pre)
        scaled_out, local_out, gain_out_grad, bias_out_grad = norm_back_local(
            pre_grad, normed_out, live, gains["gain_out"]
        )
        state = replace(replace(replace(state, 5, scaled_out), 6, normed_out), 7, pre_grad)
        grad_vec = pack_some(
            3, {"gain_out": gain_out_grad, "bias_out": bias_out_grad, "head": head_grad}
        )
        return (replace(state, 10, grad_vec), pad_pair(local_out))

    def back_fourth_middle(received, kept, stats, micro, state, totals):
        info = micro_geometry(micro)
        live = info[1]
        pieces = params[3]
        hidden_four = kept[:, :MID]
        sixth_grad = norm_back_finish(
            state[5], state[6], totals[:, :COUT], stats[1], out_counts[micro], live
        ).astype(jnp.bfloat16)
        hidden_four_grad = dense(sixth_grad, pieces["conv_out"].T).astype(jnp.bfloat16)
        leaving = pad_columns([hidden_four_grad, state[7].astype(jnp.bfloat16)])
        grad_vec = state[10] + pack_some(3, {"conv_out": outer(hidden_four, sixth_grad)})
        return (replace(replace(state, 9, leaving), 10, grad_vec), zero_local)

    backward_open = [back_first_open, back_second_open, back_third_open, back_fourth_open]
    backward_middle = [back_first_middle, back_second_middle, back_third_middle, back_fourth_middle]
    backward_close = [back_first_close, back_pass, back_third_close, back_pass]

    def backward_blank():
        return (
            jnp.zeros((in_rows, MID), jnp.float32),
            jnp.zeros((in_rows, MID), jnp.float32),
            jnp.zeros((out_rows, MID), jnp.float32),
            jnp.zeros((out_rows, MID), jnp.float32),
            jnp.zeros((out_rows, MID), jnp.float32),
            jnp.zeros((out_rows, COUT), jnp.float32),
            jnp.zeros((out_rows, COUT), jnp.float32),
            jnp.zeros((out_rows, COUT), jnp.float32),
            jnp.zeros((out_rows, COUT), jnp.float32),
            jnp.zeros((out_rows, wide), jnp.bfloat16),
            jnp.zeros((GRAD_LEN,), jnp.float32),
            jnp.zeros((in_rows, channels), jnp.float32),
        )

    steps = MICRO + phases - 1
    step_numbers = jnp.arange(steps, dtype=jnp.int32)

    def forward_step(carry, step):
        kept_inputs, kept_stats, arriving = carry
        micro_raw = step - phase
        active = (micro_raw >= 0) & (micro_raw < MICRO)
        micro = jnp.clip(micro_raw, 0, MICRO - 1)
        state, local = lax.switch(phase, forward_open, arriving, micro, forward_blank(), zero_local)
        totals = norm_totals(local)
        state, local = lax.switch(phase, forward_middle, arriving, micro, state, totals)
        totals = norm_totals(local)
        state, local = lax.switch(phase, forward_close, arriving, micro, state, totals)
        leaving, stats = (state[4], state[5])
        kept_inputs = kept_inputs.at[micro].set(jnp.where(active, arriving, kept_inputs[micro]))
        kept_stats = kept_stats.at[micro].set(jnp.where(active, stats, kept_stats[micro]))
        arriving = jax.tree.map(
            lambda part, own: part.astype(own.dtype), shifted(as_sent(leaving), "phase", 1), leaving
        )
        return ((kept_inputs, kept_stats, arriving), None)

    start_forward = (
        jnp.zeros((MICRO, out_rows, wide), jnp.bfloat16),
        jnp.zeros((MICRO, 4, COUT), jnp.float32),
        jnp.zeros((out_rows, wide), jnp.bfloat16),
    )
    forward_done, unused_forward = lax.scan(forward_step, start_forward, step_numbers)
    kept_inputs, kept_stats = (forward_done[0], forward_done[1])

    def backward_step(carry, step):
        gradient_total, input_grads, arriving = carry
        micro_raw = step - (phases - 1 - phase)
        active = (micro_raw >= 0) & (micro_raw < MICRO)
        micro = jnp.clip(micro_raw, 0, MICRO - 1)
        kept = kept_inputs[micro]
        stats = kept_stats[micro]
        state, local = lax.switch(
            phase, backward_open, arriving, kept, stats, micro, backward_blank(), zero_local
        )
        totals = norm_back_totals(local)
        state, local = lax.switch(
            phase, backward_middle, arriving, kept, stats, micro, state, totals
        )
        totals = norm_back_totals(local)
        state, local = lax.switch(
            phase, backward_close, arriving, kept, stats, micro, state, totals
        )
        leaving, contribution, input_piece = (state[9], state[10], state[11])
        gradient_total = gradient_total + jnp.where(active, contribution, 0.0)
        input_grads = input_grads.at[micro].add(jnp.where(active, input_piece, 0.0))
        arriving = jax.tree.map(
            lambda part, own: part.astype(own.dtype),
            shifted(as_sent(leaving), "phase", -1),
            leaving,
        )
        return ((gradient_total, input_grads, arriving), None)

    start_backward = (
        jnp.zeros((GRAD_LEN,), jnp.float32),
        jnp.zeros((MICRO, in_rows, channels), jnp.float32),
        jnp.zeros((out_rows, wide), jnp.bfloat16),
    )
    backward_done, unused_backward = lax.scan(backward_step, start_backward, step_numbers)
    gradient_total, input_grads = (backward_done[0], backward_done[1])
    summed = lax.psum(gradient_total, "batch")
    owned = lax.psum_scatter(
        input_grads.reshape(MICRO * in_rows, channels).astype(jnp.bfloat16),
        "phase",
        scatter_dimension=0,
        tiled=True,
    )
    return (summed[None, :], owned)


def solution(mesh):
    placed = (
        P("batch", None),
        P("phase", None),
        P(),
        P("batch", None, None),
        P("batch", None, None, None),
        P(),
        P(),
    )
    return jax.shard_map(
        shards,
        mesh=mesh,
        in_specs=placed,
        out_specs=(P("phase", None), P(("batch", "phase"), None)),
        check_vma=False,
    )
```

profile of v0, /device:TPU:0, one launch (start us, length us, event | category | flops | bytes accessed | tf_op | source)
XLA Modules:
  0.0 5196.1 jit_solution(17229189146176709226)
XLA Ops:
  34.8 1362.1 %while.47 = (s32[]{:T(128)}, bf16[4,2000,640]{2,1,0:T(8,128)(2,1)}, f32[4,4,512]{2,1,0:T(4,128)}, bf16[2000,640]{1,0:T(8,128)(2,1)S(1)}, s32[7]{0:T(128)S(1)}, /...) while((s32[]{:T(128)}, bf16[4,2000,640]{2,1,0:T(8,128)(2,1)}, ...), condition=%wide.region_48.52_spmd, body=%wide.region_1.51_spmd.sunk | while | flops 1413276160 | bytes 153618336 | solution.py:675
  1410.2 3607.9 %while.48 = (s32[]{:T(128)}, f32[213504]{0:T(1024)}, f32[4,8000,256]{2,1,0:T(8,128)}, bf16[2000,640]{1,0:T(8,128)(2,1)}, s32[7]{0:T(128)S(1)}, /*index=5*/s32[]{...) while((s32[]{:T(128)}, f32[213504]{0:T(1024)}, ...), condition=%wide.region_135.139_spmd.clone, body=%wide.region_49.138_spmd.clone.sunk | while | flops 3799219200 | bytes 349097664 | solution.py:711
  1424.1 117.9 %conditional.18 = (f32[8000,128]{1,0:T(8,128)}, f32[2000,128]{1,0:T(8,128)}, f32[2000,128]{1,0:T(8,128)}, f32[2000,128]{1,0:T(8,128)S(1)}, f32[2000,512]{1,0:T(8...) conditional(s32[]{:T(128)} %get-tuple-element.3141, ...), branch_computations={%region_50.61_spmd, %region_59.73_spmd, %region_71.82_spmd, %regio... | conditional | flops 1134322176 | bytes 97168960 | solution.py:685
  1556.0 255.9 %conditional.19 = (f32[8000,128]{1,0:T(8,128)}, f32[2000,128]{1,0:T(8,128)}, bf16[2000,640]{1,0:T(8,128)(2,1)}, f32[213504]{0:T(1024)}, f32[2,1024]{1,0:T(2,128)S(1)}) conditional(s32[]{:T(128)} %get-tuple-element.3141, (s32[]{:T(128)}, s32[4,5]{1,0:T(4,128)S(1)}, f32[4,512]{1,0:T(4,128)S(1)}, ...), branch_computations={%region_92.105_spmd, %region_103.110_spmd, %region_108.120_spmd, %... | conditional | flops 1598750720 | bytes 143842688 | solution.py:689
  1586.7 117.5 %scatter_custom_fusion.3 = f32[8000,128]{1,0:T(8,128)} fusion(s32[18000]{0:T(1024)S(1)} %reshape.6166, f32[18000,128]{1,0:T(8,128)} %reshape.5956, f32[18000]{0:T(1024)S(1)} %reshape.6019, f32[]{:T(128)} %constant.1168.clone), kind=kCustom, calls=%fused_computation.657 | custom fusion | flops 4608000 | bytes 13385732 | tf_op jit(solution)/shard_map/while/body/eval_jaxpr/cond/branch_0_fun/scatter-add | solution.py:145
  1937.9 118.1 %conditional.18 = (f32[8000,128]{1,0:T(8,128)}, f32[2000,128]{1,0:T(8,128)}, f32[2000,128]{1,0:T(8,128)}, f32[2000,128]{1,0:T(8,128)S(1)}, f32[2000,512]{1,0:T(8...) conditional(s32[]{:T(128)} %get-tuple-element.3141, ...), branch_computations={%region_50.61_spmd, %region_59.73_spmd, %region_71.82_spmd, %regio... | conditional | flops 1134322176 | bytes 97168960 | solution.py:685
  2069.9 256.0 %conditional.19 = (f32[8000,128]{1,0:T(8,128)}, f32[2000,128]{1,0:T(8,128)}, bf16[2000,640]{1,0:T(8,128)(2,1)}, f32[213504]{0:T(1024)}, f32[2,1024]{1,0:T(2,128)S(1)}) conditional(s32[]{:T(128)} %get-tuple-element.3141, (s32[]{:T(128)}, s32[4,5]{1,0:T(4,128)S(1)}, f32[4,512]{1,0:T(4,128)S(1)}, ...), branch_computations={%region_92.105_spmd, %region_103.110_spmd, %region_108.120_spmd, %... | conditional | flops 1598750720 | bytes 143842688 | solution.py:689
  2100.7 117.5 %scatter_custom_fusion.3 = f32[8000,128]{1,0:T(8,128)} fusion(s32[18000]{0:T(1024)S(1)} %reshape.6166, f32[18000,128]{1,0:T(8,128)} %reshape.5956, f32[18000]{0:T(1024)S(1)} %reshape.6019, f32[]{:T(128)} %constant.1168.clone), kind=kCustom, calls=%fused_computation.657 | custom fusion | flops 4608000 | bytes 13385732 | tf_op jit(solution)/shard_map/while/body/eval_jaxpr/cond/branch_0_fun/scatter-add | solution.py:145
  2451.9 118.1 %conditional.18 = (f32[8000,128]{1,0:T(8,128)}, f32[2000,128]{1,0:T(8,128)}, f32[2000,128]{1,0:T(8,128)}, f32[2000,128]{1,0:T(8,128)S(1)}, f32[2000,512]{1,0:T(8...) conditional(s32[]{:T(128)} %get-tuple-element.3141, ...), branch_computations={%region_50.61_spmd, %region_59.73_spmd, %region_71.82_spmd, %regio... | conditional | flops 1134322176 | bytes 97168960 | solution.py:685
  2583.9 256.0 %conditional.19 = (f32[8000,128]{1,0:T(8,128)}, f32[2000,128]{1,0:T(8,128)}, bf16[2000,640]{1,0:T(8,128)(2,1)}, f32[213504]{0:T(1024)}, f32[2,1024]{1,0:T(2,128)S(1)}) conditional(s32[]{:T(128)} %get-tuple-element.3141, (s32[]{:T(128)}, s32[4,5]{1,0:T(4,128)S(1)}, f32[4,512]{1,0:T(4,128)S(1)}, ...), branch_computations={%region_92.105_spmd, %region_103.110_spmd, %region_108.120_spmd, %... | conditional | flops 1598750720 | bytes 143842688 | solution.py:689
  2614.7 117.5 %scatter_custom_fusion.3 = f32[8000,128]{1,0:T(8,128)} fusion(s32[18000]{0:T(1024)S(1)} %reshape.6166, f32[18000,128]{1,0:T(8,128)} %reshape.5956, f32[18000]{0:T(1024)S(1)} %reshape.6019, f32[]{:T(128)} %constant.1168.clone), kind=kCustom, calls=%fused_computation.657 | custom fusion | flops 4608000 | bytes 13385732 | tf_op jit(solution)/shard_map/while/body/eval_jaxpr/cond/branch_0_fun/scatter-add | solution.py:145
  2965.8 118.1 %conditional.18 = (f32[8000,128]{1,0:T(8,128)}, f32[2000,128]{1,0:T(8,128)}, f32[2000,128]{1,0:T(8,128)}, f32[2000,128]{1,0:T(8,128)S(1)}, f32[2000,512]{1,0:T(8...) conditional(s32[]{:T(128)} %get-tuple-element.3141, ...), branch_computations={%region_50.61_spmd, %region_59.73_spmd, %region_71.82_spmd, %regio... | conditional | flops 1134322176 | bytes 97168960 | solution.py:685
  3097.9 256.0 %conditional.19 = (f32[8000,128]{1,0:T(8,128)}, f32[2000,128]{1,0:T(8,128)}, bf16[2000,640]{1,0:T(8,128)(2,1)}, f32[213504]{0:T(1024)}, f32[2,1024]{1,0:T(2,128)S(1)}) conditional(s32[]{:T(128)} %get-tuple-element.3141, (s32[]{:T(128)}, s32[4,5]{1,0:T(4,128)S(1)}, f32[4,512]{1,0:T(4,128)S(1)}, ...), branch_computations={%region_92.105_spmd, %region_103.110_spmd, %region_108.120_spmd, %... | conditional | flops 1598750720 | bytes 143842688 | solution.py:689
  3128.6 117.5 %scatter_custom_fusion.3 = f32[8000,128]{1,0:T(8,128)} fusion(s32[18000]{0:T(1024)S(1)} %reshape.6166, f32[18000,128]{1,0:T(8,128)} %reshape.5956, f32[18000]{0:T(1024)S(1)} %reshape.6019, f32[]{:T(128)} %constant.1168.clone), kind=kCustom, calls=%fused_computation.657 | custom fusion | flops 4608000 | bytes 13385732 | tf_op jit(solution)/shard_map/while/body/eval_jaxpr/cond/branch_0_fun/scatter-add | solution.py:145
  3479.8 118.1 %conditional.18 = (f32[8000,128]{1,0:T(8,128)}, f32[2000,128]{1,0:T(8,128)}, f32[2000,128]{1,0:T(8,128)}, f32[2000,128]{1,0:T(8,128)S(1)}, f32[2000,512]{1,0:T(8...) conditional(s32[]{:T(128)} %get-tuple-element.3141, ...), branch_computations={%region_50.61_spmd, %region_59.73_spmd, %region_71.82_spmd, %regio... | conditional | flops 1134322176 | bytes 97168960 | solution.py:685
  3611.9 256.0 %conditional.19 = (f32[8000,128]{1,0:T(8,128)}, f32[2000,128]{1,0:T(8,128)}, bf16[2000,640]{1,0:T(8,128)(2,1)}, f32[213504]{0:T(1024)}, f32[2,1024]{1,0:T(2,128)S(1)}) conditional(s32[]{:T(128)} %get-tuple-element.3141, (s32[]{:T(128)}, s32[4,5]{1,0:T(4,128)S(1)}, f32[4,512]{1,0:T(4,128)S(1)}, ...), branch_computations={%region_92.105_spmd, %region_103.110_spmd, %region_108.120_spmd, %... | conditional | flops 1598750720 | bytes 143842688 | solution.py:689
  3642.6 117.5 %scatter_custom_fusion.3 = f32[8000,128]{1,0:T(8,128)} fusion(s32[18000]{0:T(1024)S(1)} %reshape.6166, f32[18000,128]{1,0:T(8,128)} %reshape.5956, f32[18000]{0:T(1024)S(1)} %reshape.6019, f32[]{:T(128)} %constant.1168.clone), kind=kCustom, calls=%fused_computation.657 | custom fusion | flops 4608000 | bytes 13385732 | tf_op jit(solution)/shard_map/while/body/eval_jaxpr/cond/branch_0_fun/scatter-add | solution.py:145
  3993.8 118.1 %conditional.18 = (f32[8000,128]{1,0:T(8,128)}, f32[2000,128]{1,0:T(8,128)}, f32[2000,128]{1,0:T(8,128)}, f32[2000,128]{1,0:T(8,128)S(1)}, f32[2000,512]{1,0:T(8...) conditional(s32[]{:T(128)} %get-tuple-element.3141, ...), branch_computations={%region_50.61_spmd, %region_59.73_spmd, %region_71.82_spmd, %regio... | conditional | flops 1134322176 | bytes 97168960 | solution.py:685
  4125.8 250.4 %conditional.19 = (f32[8000,128]{1,0:T(8,128)}, f32[2000,128]{1,0:T(8,128)}, bf16[2000,640]{1,0:T(8,128)(2,1)}, f32[213504]{0:T(1024)}, f32[2,1024]{1,0:T(2,128)S(1)}) conditional(s32[]{:T(128)} %get-tuple-element.3141, (s32[]{:T(128)}, s32[4,5]{1,0:T(4,128)S(1)}, f32[4,512]{1,0:T(4,128)S(1)}, ...), branch_computations={%region_92.105_spmd, %region_103.110_spmd, %region_108.120_spmd, %... | conditional | flops 1598750720 | bytes 143842688 | solution.py:689
  4156.6 112.0 %scatter_custom_fusion.3 = f32[8000,128]{1,0:T(8,128)} fusion(s32[18000]{0:T(1024)S(1)} %reshape.6166, f32[18000,128]{1,0:T(8,128)} %reshape.5956, f32[18000]{0:T(1024)S(1)} %reshape.6019, f32[]{:T(128)} %constant.1168.clone), kind=kCustom, calls=%fused_computation.657 | custom fusion | flops 4608000 | bytes 13385732 | tf_op jit(solution)/shard_map/while/body/eval_jaxpr/cond/branch_0_fun/scatter-add | solution.py:145
  4507.5 118.1 %conditional.18 = (f32[8000,128]{1,0:T(8,128)}, f32[2000,128]{1,0:T(8,128)}, f32[2000,128]{1,0:T(8,128)}, f32[2000,128]{1,0:T(8,128)S(1)}, f32[2000,512]{1,0:T(8...) conditional(s32[]{:T(128)} %get-tuple-element.3141, ...), branch_computations={%region_50.61_spmd, %region_59.73_spmd, %region_71.82_spmd, %regio... | conditional | flops 1134322176 | bytes 97168960 | solution.py:685
  4639.5 256.0 %conditional.19 = (f32[8000,128]{1,0:T(8,128)}, f32[2000,128]{1,0:T(8,128)}, bf16[2000,640]{1,0:T(8,128)(2,1)}, f32[213504]{0:T(1024)}, f32[2,1024]{1,0:T(2,128)S(1)}) conditional(s32[]{:T(128)} %get-tuple-element.3141, (s32[]{:T(128)}, s32[4,5]{1,0:T(4,128)S(1)}, f32[4,512]{1,0:T(4,128)S(1)}, ...), branch_computations={%region_92.105_spmd, %region_103.110_spmd, %region_108.120_spmd, %... | conditional | flops 1598750720 | bytes 143842688 | solution.py:689
  4670.2 117.5 %scatter_custom_fusion.3 = f32[8000,128]{1,0:T(8,128)} fusion(s32[18000]{0:T(1024)S(1)} %reshape.6166, f32[18000,128]{1,0:T(8,128)} %reshape.5956, f32[18000]{0:T(1024)S(1)} %reshape.6019, f32[]{:T(128)} %constant.1168.clone), kind=kCustom, calls=%fused_computation.657 | custom fusion | flops 4608000 | bytes 13385732 | tf_op jit(solution)/shard_map/while/body/eval_jaxpr/cond/branch_0_fun/scatter-add | solution.py:145
  5075.4 111.0 %reduce-scatter.2.cloned.1.call-done = bf16[8000,256]{1,0:T(8,128)(2,1)} async-done(((bf16[32000,256]{1,0:T(8,128)(2,1)}), bf16[8000,256]{1,0:T(8,128)(2,1)}) %reduce-scatter.2.cloned.1.call-update) | async-done | bytes 4096016 | tf_op jit(solution)/shard_map/reduce_scatter | solution.py:714
  (1752 shorter events, 4893.1 us)
Async XLA Ops:
  8.0 5067.4 %all-reduce.25.cloned.1.call-start = ((), (), s32[]{:S(2)}) async-start(), calls=%async_computation.1 | async-start | bytes 1708032 | tf_op jit(solution)/shard_map/psum | solution.py:713
  193.4 56.7 %collective-permute-start = (bf16[2000,640]{1,0:T(8,128)(2,1)}, bf16[2000,640]{1,0:T(8,128)(2,1)}, u32[]{:S(2)}, u32[]{:S(2)}) collective-permute-start(bf16[2000,640]{1,0:T(8,128)(2,1)} %get-tuple-element.2754), channel_id=1, source_target_pairs={{0,8},{8,16},{16,24},{1,9},{9,17},{17,25},{2,10},{10,18},{18,26},{... | collective-permute-start | bytes 7680008 | tf_op jit(solution)/shard_map/while/body/eval_jaxpr/ppermute | solution.py:33
  384.2 56.8 %collective-permute-start = (bf16[2000,640]{1,0:T(8,128)(2,1)}, bf16[2000,640]{1,0:T(8,128)(2,1)}, u32[]{:S(2)}, u32[]{:S(2)}) collective-permute-start(bf16[2000,640]{1,0:T(8,128)(2,1)} %get-tuple-element.2754), channel_id=1, source_target_pairs={{0,8},{8,16},{16,24},{1,9},{9,17},{17,25},{2,10},{10,18},{18,26},{... | collective-permute-start | bytes 7680008 | tf_op jit(solution)/shard_map/while/body/eval_jaxpr/ppermute | solution.py:33
  575.1 56.7 %collective-permute-start = (bf16[2000,640]{1,0:T(8,128)(2,1)}, bf16[2000,640]{1,0:T(8,128)(2,1)}, u32[]{:S(2)}, u32[]{:S(2)}) collective-permute-start(bf16[2000,640]{1,0:T(8,128)(2,1)} %get-tuple-element.2754), channel_id=1, source_target_pairs={{0,8},{8,16},{16,24},{1,9},{9,17},{17,25},{2,10},{10,18},{18,26},{... | collective-permute-start | bytes 7680008 | tf_op jit(solution)/shard_map/while/body/eval_jaxpr/ppermute | solution.py:33
  765.8 56.8 %collective-permute-start = (bf16[2000,640]{1,0:T(8,128)(2,1)}, bf16[2000,640]{1,0:T(8,128)(2,1)}, u32[]{:S(2)}, u32[]{:S(2)}) collective-permute-start(bf16[2000,640]{1,0:T(8,128)(2,1)} %get-tuple-element.2754), channel_id=1, source_target_pairs={{0,8},{8,16},{16,24},{1,9},{9,17},{17,25},{2,10},{10,18},{18,26},{... | collective-permute-start | bytes 7680008 | tf_op jit(solution)/shard_map/while/body/eval_jaxpr/ppermute | solution.py:33
  956.7 56.7 %collective-permute-start = (bf16[2000,640]{1,0:T(8,128)(2,1)}, bf16[2000,640]{1,0:T(8,128)(2,1)}, u32[]{:S(2)}, u32[]{:S(2)}) collective-permute-start(bf16[2000,640]{1,0:T(8,128)(2,1)} %get-tuple-element.2754), channel_id=1, source_target_pairs={{0,8},{8,16},{16,24},{1,9},{9,17},{17,25},{2,10},{10,18},{18,26},{... | collective-permute-start | bytes 7680008 | tf_op jit(solution)/shard_map/while/body/eval_jaxpr/ppermute | solution.py:33
  1147.5 56.8 %collective-permute-start = (bf16[2000,640]{1,0:T(8,128)(2,1)}, bf16[2000,640]{1,0:T(8,128)(2,1)}, u32[]{:S(2)}, u32[]{:S(2)}) collective-permute-start(bf16[2000,640]{1,0:T(8,128)(2,1)} %get-tuple-element.2754), channel_id=1, source_target_pairs={{0,8},{8,16},{16,24},{1,9},{9,17},{17,25},{2,10},{10,18},{18,26},{... | collective-permute-start | bytes 7680008 | tf_op jit(solution)/shard_map/while/body/eval_jaxpr/ppermute | solution.py:33
  1338.4 56.7 %collective-permute-start = (bf16[2000,640]{1,0:T(8,128)(2,1)}, bf16[2000,640]{1,0:T(8,128)(2,1)}, u32[]{:S(2)}, u32[]{:S(2)}) collective-permute-start(bf16[2000,640]{1,0:T(8,128)(2,1)} %get-tuple-element.2754), channel_id=1, source_target_pairs={{0,8},{8,16},{16,24},{1,9},{9,17},{17,25},{2,10},{10,18},{18,26},{... | collective-permute-start | bytes 7680008 | tf_op jit(solution)/shard_map/while/body/eval_jaxpr/ppermute | solution.py:33
  1871.1 59.4 %collective-permute-start.1 = (bf16[2000,640]{1,0:T(8,128)(2,1)}, bf16[2000,640]{1,0:T(8,128)(2,1)S(1)}, u32[]{:S(2)}, u32[]{:S(2)}) collective-permute-start(bf16[2000,640]{1,0:T(8,128)(2,1)} %get-tuple-element.2807), channel_id=1, source_target_pairs={{8,0},{16,8},{24,16},{9,1},{17,9},{25,17},{10,2},{18,10},{26,18},{... | collective-permute-start | bytes 7680008 | tf_op jit(solution)/shard_map/while/body/eval_jaxpr/ppermute | solution.py:33
  1873.6 58.4 %copy-start.49 = (f32[512]{0:T(512)S(1)}, f32[512]{0:T(512)}, u32[]{:S(2)}) copy-start(f32[512]{0:T(512)} %copy-done.48) | copy-start | bytes 6148 | tf_op jit(solution)/shard_map/while
  2385.1 59.4 %collective-permute-start.1 = (bf16[2000,640]{1,0:T(8,128)(2,1)}, bf16[2000,640]{1,0:T(8,128)(2,1)S(1)}, u32[]{:S(2)}, u32[]{:S(2)}) collective-permute-start(bf16[2000,640]{1,0:T(8,128)(2,1)} %get-tuple-element.2807), channel_id=1, source_target_pairs={{8,0},{16,8},{24,16},{9,1},{17,9},{25,17},{10,2},{18,10},{26,18},{... | collective-permute-start | bytes 7680008 | tf_op jit(solution)/shard_map/while/body/eval_jaxpr/ppermute | solution.py:33
  2899.1 59.4 %collective-permute-start.1 = (bf16[2000,640]{1,0:T(8,128)(2,1)}, bf16[2000,640]{1,0:T(8,128)(2,1)S(1)}, u32[]{:S(2)}, u32[]{:S(2)}) collective-permute-start(bf16[2000,640]{1,0:T(8,128)(2,1)} %get-tuple-element.2807), channel_id=1, source_target_pairs={{8,0},{16,8},{24,16},{9,1},{17,9},{25,17},{10,2},{18,10},{26,18},{... | collective-permute-start | bytes 7680008 | tf_op jit(solution)/shard_map/while/body/eval_jaxpr/ppermute | solution.py:33
  2901.6 58.4 %copy-start.45 = (bf16[256,128]{1,0:T(8,128)(2,1)S(1)}, bf16[256,128]{1,0:T(8,128)(2,1)}, u32[]{:S(2)}) copy-start(bf16[256,128]{1,0:T(8,128)(2,1)} %copy-done.44) | copy-start | bytes 196612 | tf_op jit(solution)/shard_map/while
  2901.6 58.4 %copy-start.49 = (f32[512]{0:T(512)S(1)}, f32[512]{0:T(512)}, u32[]{:S(2)}) copy-start(f32[512]{0:T(512)} %copy-done.48) | copy-start | bytes 6148 | tf_op jit(solution)/shard_map/while
  2901.6 58.4 %copy-start.51 = (f32[512]{0:T(512)S(1)}, f32[512]{0:T(512)}, u32[]{:S(2)}) copy-start(f32[512]{0:T(512)} %get-tuple-element.3252) | copy-start | bytes 6148 | tf_op jit(solution)/shard_map/while
  2901.6 58.4 %copy-start.56 = (f32[512]{0:T(512)S(1)}, f32[512]{0:T(512)}, u32[]{:S(2)}) copy-start(f32[512]{0:T(512)} %get-tuple-element.3298) | copy-start | bytes 6148 | tf_op jit(solution)/shard_map/while
  2901.6 58.4 %copy-start.58 = (f32[128]{0:T(128)S(1)}, f32[128]{0:T(128)}, u32[]{:S(2)}) copy-start(f32[128]{0:T(128)} %get-tuple-element.3344) | copy-start | bytes 1540 | tf_op jit(solution)/shard_map/while
  2901.6 58.4 %copy-start.66 = (f32[128]{0:T(128)S(1)}, f32[128]{0:T(128)}, u32[]{:S(2)}) copy-start(f32[128]{0:T(128)} %get-tuple-element.3395) | copy-start | bytes 1540 | tf_op jit(solution)/shard_map/while
  2901.6 58.4 %copy-start.81 = (s32[7]{0:T(128)S(1)}, s32[7]{0:T(128)}, u32[]{:S(2)}) copy-start(s32[7]{0:T(128)} %copy-done.80) | copy-start | bytes 88 | tf_op jit(solution)/shard_map/while
  3413.0 59.4 %collective-permute-start.1 = (bf16[2000,640]{1,0:T(8,128)(2,1)}, bf16[2000,640]{1,0:T(8,128)(2,1)S(1)}, u32[]{:S(2)}, u32[]{:S(2)}) collective-permute-start(bf16[2000,640]{1,0:T(8,128)(2,1)} %get-tuple-element.2807), channel_id=1, source_target_pairs={{8,0},{16,8},{24,16},{9,1},{17,9},{25,17},{10,2},{18,10},{26,18},{... | collective-permute-start | bytes 7680008 | tf_op jit(solution)/shard_map/while/body/eval_jaxpr/ppermute | solution.py:33
  3927.1 59.3 %collective-permute-start.1 = (bf16[2000,640]{1,0:T(8,128)(2,1)}, bf16[2000,640]{1,0:T(8,128)(2,1)S(1)}, u32[]{:S(2)}, u32[]{:S(2)}) collective-permute-start(bf16[2000,640]{1,0:T(8,128)(2,1)} %get-tuple-element.2807), channel_id=1, source_target_pairs={{8,0},{16,8},{24,16},{9,1},{17,9},{25,17},{10,2},{18,10},{26,18},{... | collective-permute-start | bytes 7680008 | tf_op jit(solution)/shard_map/while/body/eval_jaxpr/ppermute | solution.py:33
  4440.7 59.4 %collective-permute-start.1 = (bf16[2000,640]{1,0:T(8,128)(2,1)}, bf16[2000,640]{1,0:T(8,128)(2,1)S(1)}, u32[]{:S(2)}, u32[]{:S(2)}) collective-permute-start(bf16[2000,640]{1,0:T(8,128)(2,1)} %get-tuple-element.2807), channel_id=1, source_target_pairs={{8,0},{16,8},{24,16},{9,1},{17,9},{25,17},{10,2},{18,10},{26,18},{... | collective-permute-start | bytes 7680008 | tf_op jit(solution)/shard_map/while/body/eval_jaxpr/ppermute | solution.py:33
  4954.7 59.3 %collective-permute-start.1 = (bf16[2000,640]{1,0:T(8,128)(2,1)}, bf16[2000,640]{1,0:T(8,128)(2,1)S(1)}, u32[]{:S(2)}, u32[]{:S(2)}) collective-permute-start(bf16[2000,640]{1,0:T(8,128)(2,1)} %get-tuple-element.2807), channel_id=1, source_target_pairs={{8,0},{16,8},{24,16},{9,1},{17,9},{25,17},{10,2},{18,10},{26,18},{... | collective-permute-start | bytes 7680008 | tf_op jit(solution)/shard_map/while/body/eval_jaxpr/ppermute | solution.py:33
  5023.0 163.5 %reduce-scatter.2.cloned.1.call-start = ((), (), s32[]{:S(2)}) async-start(), calls=%async_computation.2 | async-start | bytes 20480000 | tf_op jit(solution)/shard_map/reduce_scatter | solution.py:714
  (259 other events, 6479.6 us)
Sparse Core Ops, SparseCore 0:
  5023.1 52.3 all-reduce.24
Sparse Core Ops, SparseCore 1:
  5040.1 146.3 reduce-scatter.1
where the time goes:
time: 5230 us; the launch traced here: 5200 us
  other arithmetic  1750 us (33%)
  local copies, waits for them, and re-layouts  1590 us (30%)
  waiting for transfers between devices  790 us (15%)
  blocking collectives  399 us (8%)
  loops' own time  396 us (8%)
  matrix products  220 us (4%)
    scatter-add x7, other arithmetic, scatter_taps(): jax.ops.segment_sum(spread.reshape(-1, channels), index.reshape(-1), num_...  817 us
    gather x21, local copies, waits for them, and re-layouts, gather_taps(): jnp.take(source, index.reshape(-1), axis=0)  779 us
    ppermute x14, waiting for transfers between devices, shifted(): return lax.ppermute(block, axis, route)  643 us
    reshape x42, local copies, waits for them, and re-layouts, gather_taps(): jnp.take(source, index.reshape(-1), axis=0)  344 us
    select_n x42, other arithmetic, gather_taps(): jnp.take(source, index.reshape(-1), axis=0)  271 us
    psum x14, blocking collectives, norm_back_totals(): return lax.psum(local, 'batch')  200 us
    psum x14, blocking collectives, norm_totals(): return lax.psum(local, 'batch')  199 us
    dot_general x42, matrix products, dense(): return jnp.dot(left, right, preferred_element_type=jnp.float32)  186 us
  transfers between devices with their start and end apart: 16, of which 16 were waited for; matrix products, arithmetic and copies ran while one was open for 3% of the time, Pallas kernels for 0%

commit v1 on v0

v1 whole, which is shorter than its diff:
```python
import functools
import math
import types

import jax
import jax.numpy as jnp
from jax import lax
from jax.experimental import pallas as pl
from jax.experimental.pallas import tpu as pltpu
from jax.sharding import PartitionSpec as P

CIN = 256
MID = 128
COUT = 512
EMB = 128
SIDE_UNIT = 4
MICRO = 4
NEG = 4096
BANK = 16384
GRAD_LEN = 213504
LANES = 128
SOFTMAX_TEMPER = 0.07
EPSILON = 1e-05

PAD = 48
ROW = GRAD_LEN // LANES
ROWS = -(-ROW // 16) * 16
BLOCK = 16
TABLE = 512
UNROLL = 5
EARLY = 272
AHEAD = 80
MESH = pl.DeviceIdType.MESH
F32 = jnp.float32
BF16 = jnp.bfloat16

IN_GAIN, IN_BIAS, MID_AT = CIN, CIN + 1, CIN + 2
MID_GAIN, MID_BIAS = MID_AT + 9 * MID, MID_AT + 9 * MID + 1
THIRD_GAIN, THIRD_BIAS, THIRD_MID = COUT, COUT + 1, COUT + 2
THIRD_MID_GAIN, THIRD_MID_BIAS = THIRD_MID + 9 * MID, THIRD_MID + 9 * MID + 1
OUT_GAIN, OUT_BIAS, AFTER_OUT = 512, 516, 520
SHORT_GAIN, SHORT_BIAS = AFTER_OUT + 1024, AFTER_OUT + 1028

EXCHANGES = 12
SPANS = {2: 16, 5: 8, 6: 8, 9: 16}
STARTS = {2: 0, 5: 16, 6: 24, 9: 32}
SPAN_ROWS = 48

PIECES = ((3, 1032), (2, 1668), (1, 1552), (0, 9 * MID), (0, 260))
LAST, THIRD, SECOND, FIRST_MID, FIRST_IN = range(5)

L1, L2, L3, LS, L4, L5, L6 = range(7)
HALF_SCALE, HALF_SHIFT, INVERSE, NEG_MEAN, GRAD_A, GRAD_E, GRAD_D = range(7)


def dense(left, right):
    return jnp.dot(left, right, preferred_element_type=F32)


def across(left, right):
    return lax.dot_general(left, right, (((1,), (1,)), ((), ())), preferred_element_type=F32)


def outer(left, right):
    return lax.dot_general(left, right, (((0,), (0,)), ((), ())), preferred_element_type=F32)


def folded(values):
    rows, width = values.shape
    return values.reshape(rows // 8, 8, width).sum(axis=0)


def silu_half(half):
    return half + half * jnp.tanh(half)


def slope_half(half):
    bend = jnp.tanh(half)
    return 0.5 * (1.0 + bend + half * (1.0 - bend * bend))


def split(values):
    high = values.astype(BF16)
    return high, (values - high.astype(F32)).astype(BF16)


def line_levels(lines):
    return [lines] if lines <= 8 else [lines // 8, 8]


def kernel(names, batches, phases, in_rows, slots, *refs):
    k = types.SimpleNamespace(**dict(zip(names, refs, strict=True)))
    out_rows = in_rows // 4
    plane = out_rows + 2 * PAD
    chunk = out_rows // 5
    part = out_rows // 25
    blocks = out_rows // BLOCK
    per = part // BLOCK
    me = lax.axis_index("batch")
    stage = lax.axis_index("phase")
    core = lax.rem(me, 2)
    line = lax.div(me, 2)
    lines = batches // 2
    group = 2 * phases
    mine = 2 * stage + core
    levels = line_levels(lines)
    half_bank = BANK // 2
    quarter = in_rows // 4
    feat, t1, big0, big1, big2, src = k.feat, k.t1, k.big0, k.big1, k.big2, k.src
    tab, masks, wst, wts, gw, wide2, gn = k.tab, k.masks, k.wst, k.wts, k.gw, k.wide2, k.gn

    def batch_peer(i):
        return {"batch": lax.rem(me + i, batches)}

    def phase_peer(i):
        return {"phase": lax.rem(stage + i, phases)}

    def remote(source, target, send_sem, recv_sem, device):
        return pltpu.make_async_remote_copy(
            src_ref=source,
            dst_ref=target,
            send_sem=send_sem,
            recv_sem=recv_sem,
            device_id=device,
            device_id_type=MESH,
        )

    def wait_for(sem, region):
        pltpu.make_async_copy(region, region, sem).wait()

    barrier = pltpu.get_barrier_semaphore()

    def greet(i, carry):
        pl.semaphore_signal(barrier, inc=1, device_id=batch_peer(i), device_id_type=MESH)
        return carry

    lax.fori_loop(1, batches, greet, 0)
    for i in range(1, phases):
        for other in (me, 2 * line + 1 - core):
            pl.semaphore_signal(
                barrier,
                inc=1,
                device_id={"phase": lax.rem(stage + i, phases), "batch": other},
                device_id_type=MESH,
            )

    raw_copy = pltpu.make_async_copy(k.weights_at, k.raw, k.raw_sem)
    raw_copy.start()
    feat_copies = []
    for i in range(4):
        copy = pltpu.make_async_copy(
            k.features_at.at[pl.ds(pl.multiple_of(stage * in_rows + i * quarter, 16), quarter)],
            feat.at[pl.ds(i * quarter, quarter)],
            k.feat_sem.at[i],
        )
        copy.start()
        feat_copies.append(copy)
    neg_copy = pltpu.make_async_copy(k.negatives_at.at[0], k.neg, k.neg_sem)
    neg_copy.start()
    bank_copies = [
        pltpu.make_async_copy(
            k.bank_at.at[pl.ds(i * half_bank, half_bank)],
            big0.at[pl.ds(0, half_bank)],
            k.bank_sem.at[i],
        )
        for i in range(2)
    ]

    def side_of(kind):
        return SIDE_UNIT * jnp.where(
            kind == 1, 5, jnp.where(kind == 2, 7, jnp.where(kind == 3, 9, 0))
        )

    sides = [side_of(k.kinds[slot, stage, me]) for slot in range(slots)]
    ends = []
    for side in sides:
        ends.append(side * side + (ends[-1] if ends else 0))
    starts = [0, *ends[:-1]]
    rows_live = ends[-1]

    def all_areas(i, carry):
        for slot in range(slots):
            side = side_of(k.kinds[slot, stage, i])
            carry = carry + side * side
        return carry

    live_pixels = lax.fori_loop(0, batches, all_areas, 0)
    inverse_count = 1.0 / jnp.full((1, LANES), live_pixels, jnp.int32).astype(F32)[:, 0:1]

    def place(first):
        base = jnp.zeros_like(first)
        width = jnp.zeros_like(first)
        slot = jnp.full_like(first, 7)
        for number in range(slots):
            inside = (first >= starts[number]) & (first < ends[number])
            base = jnp.where(inside, starts[number], base)
            width = jnp.where(inside, sides[number], width)
            slot = jnp.where(inside, number, slot)
        return base, width, slot

    def divided(value, side):
        factor = jnp.zeros_like(side)
        for kind in (5, 7, 9):
            factor = jnp.where(side == SIDE_UNIT * kind, 65536 // (SIDE_UNIT * kind) + 1, factor)
        return lax.shift_right_logical(value * factor, jnp.full_like(value, 16))

    index = lax.broadcasted_iota(jnp.int32, (1, TABLE), 1)
    first = BLOCK * index
    base, width, slot = place(first)
    live = width > 0
    local = jnp.where(live, first - base, 0)
    row = divided(local, width)
    left = jnp.where(live, (row + 1) * width - local, BLOCK)
    begin = jnp.where(live, 4 * base + 2 * (local + row * width), 4 * first)
    jump = jnp.where(left < BLOCK, 2 * width, 0)
    window_at = lax.shift_right_logical(
        index * (65536 // per + 1), jnp.full_like(index, 16)
    ) * (4 * part) - AHEAD
    in_window = begin - jnp.maximum(window_at, 0)
    pixel = BLOCK // 4 * index
    in_base, in_width, unused_slot = place(pixel)
    in_live = in_width > 0
    in_side = jnp.maximum(in_width, 1)
    in_local = 4 * (pixel - in_base)
    in_row = divided(2 * (pixel - in_base), in_width)
    in_left = jnp.where(in_live, (2 * in_side - (in_local - in_row * 2 * in_side)) >> 1, 8)
    upper = in_row >> 1
    odd = in_row - 2 * upper
    lower = (in_row + 1) >> 1
    here = in_base + upper * in_side + (in_side - in_left)
    below = in_base + lower * in_side - in_left
    at_here = jnp.where(in_live, PAD + here + odd * (2 * plane), PAD + out_rows - BLOCK)
    at_below = jnp.where(in_left < 8, PAD + below + (1 - odd) * (2 * plane), at_here)
    even_here = jnp.where(in_live & (odd == 0), PAD + here, 0)
    even_below = jnp.where(in_live & (in_left < 8) & (odd == 1), PAD + below, 0)
    columns = (width, local, begin, left, jump, slot, 2 * width)
    columns = columns + (at_here, at_below, in_left, even_here, even_below, in_window)
    for number, column in enumerate(columns):
        k.tabv[number : number + 1, :] = column
    tab_copy = pltpu.make_async_copy(k.tabv, tab, k.tab_sem)
    tab_copy.start()

    raw_copy.wait()

    def to_rows(first, last):
        def body(i, carry):
            found = []
            for u in range(16):
                at = pl.multiple_of((i * 16 + u) * LANES, LANES)
                found.append(k.raw[0:1, pl.ds(at, LANES)].astype(F32))
            for u, values in enumerate(found):
                wst[pl.ds(i * 16 + u, 1), :] = values
            return carry

        lax.fori_loop(first // 16, last // 16, body, 0)
        done = last // 16 * 16
        for at in range(done, last):
            wst[at : at + 1, :] = k.raw[0:1, at * LANES : (at + 1) * LANES].astype(F32)
        if done < last:
            wst[last : done + 16, :] = jnp.zeros((done + 16 - last, LANES), F32)

        def convert(i, carry):
            rows = pl.ds(pl.multiple_of(i * 16, 16), 16)
            wts[stage, rows, :] = wst[rows, :].astype(BF16)
            return carry

        lax.fori_loop(first // 16, -(-last // 16), convert, 0, unroll=2)

    weight_spans = ((0, EARLY), (EARLY, ROWS - EARLY))

    def send_weights(number):
        at, rows = weight_spans[number]
        region = wts.at[stage, pl.ds(at, rows)]
        copies = []
        for i in range(1, phases):
            copy = remote(
                region,
                region,
                k.weight_send.at[number, i],
                k.weight_recv.at[number, stage],
                phase_peer(i),
            )
            copy.start()
            copies.append(copy)
        return copies

    def need_weights(number, section):
        at, rows = weight_spans[number]

        @pl.when(stage != section)
        def unused_wait():
            wait_for(k.weight_recv.at[number, section], wts.at[section, pl.ds(at, rows)])

    to_rows(0, EARLY)
    pl.semaphore_wait(barrier, batches - 1 + 2 * (phases - 1))
    weight_copies = send_weights(0)

    def outgoing(number):
        if number in SPANS:
            return k.send.at[pl.ds(STARTS[number], SPANS[number])]
        return k.send_narrow.at[number]

    def incoming(number, which):
        if number in SPANS:
            return k.recv.at[which, pl.ds(STARTS[number], SPANS[number])]
        return k.recv_narrow.at[number, which]

    def share(number):
        def give(i, carry):
            remote(
                outgoing(number),
                incoming(number, me),
                k.stat_send.at[number],
                k.stat_recv.at[number],
                batch_peer(i),
            ).start()
            return carry

        lax.fori_loop(1, batches, give, 0, unroll=batches <= 8)
        incoming(number, me)[...] = outgoing(number)[...]

    def collect(number):
        wait_for(k.stat_recv.at[number], incoming(number, pl.ds(0, batches - 1)))

        def add(i, carry):
            return carry + incoming(number, i)[...]

        rows = SPANS.get(number, 2)
        k.total[pl.ds(0, rows), :] = lax.fori_loop(
            1, batches, add, incoming(number, 0)[...], unroll=batches <= 8
        )

    padded = [-(-rows // (16 * group)) * 16 * group for unused, rows in PIECES]
    piece_at = [sum(padded[:i]) for i in range(len(padded))]
    section_at = [0, 0, 0, 0, padded[FIRST_MID]]
    part_of = [rows // group for rows in padded]

    def summed(rows, target, *sources):
        total = sources[0](0, rows).astype(F32)
        for source in sources[1:]:
            total = total + source(0, rows).astype(F32)
        target(0, rows, total.astype(BF16))

    def reader(ref, start):
        return lambda at, step: ref[pl.ds(pl.multiple_of(start + at, 16), step), :]

    def writer(ref, start):
        def write(at, step, values):
            ref[pl.ds(pl.multiple_of(start + at, 16), step), :] = values

        return write

    def give_scatter(number):
        rows, at = part_of[number], piece_at[number]

        def give(i, carry):
            other = lax.rem(mine + i, group)
            remote(
                k.gb.at[pl.ds(at + other * rows, rows)],
                k.got_scatter.at[i - 1, pl.ds(at // group, rows)],
                k.scatter_send.at[number],
                k.scatter_recv.at[number],
                {"phase": lax.div(other, 2), "batch": 2 * line + lax.rem(other, 2)},
            ).start()
            return carry

        lax.fori_loop(1, group, give, 0)

    def give_line(number):
        rows, at = part_of[number], piece_at[number]
        within = at // group
        wait_for(k.scatter_recv.at[number], k.got_scatter.at[:, pl.ds(within, rows)])

        def other(i):
            return lambda start, step: k.got_scatter[i, pl.ds(within + start, step), :]

        summed(
            rows,
            writer(k.line_sum.at[0], within),
            reader(k.gb, at + mine * rows),
            *[other(i) for i in range(group - 1)],
        )
        send_level(number, 0)

    def level_of(level):
        size, stride = levels[level], math.prod(levels[:level])
        return size, stride, sum(levels[:level]) - level, lax.rem(lax.div(line, stride), size)

    def send_level(number, level):
        size, stride, slot, digit = level_of(level)
        rows, within = part_of[number], piece_at[number] // group

        def give(i, carry):
            other = line + (lax.rem(digit + i, size) - digit) * stride
            remote(
                k.line_sum.at[level, pl.ds(within, rows)],
                k.got_line.at[slot + i - 1, pl.ds(within, rows)],
                k.line_send.at[level, number],
                k.line_recv.at[level, number],
                {"batch": 2 * other + core},
            ).start()
            return carry

        lax.fori_loop(1, size, give, 0)

    def add_level(number, level, target):
        size, stride, slot, digit = level_of(level)
        rows, within = part_of[number], piece_at[number] // group
        arrived = k.got_line.at[pl.ds(slot, size - 1), pl.ds(within, rows)]
        wait_for(k.line_recv.at[level, number], arrived)

        own = k.line_sum[level, pl.ds(within, rows), :].astype(F32)
        total = jnp.zeros((rows, LANES), F32)
        for which in range(size):
            at = jnp.minimum(lax.rem(digit - which - 1 + size, size), size - 2)
            found = k.got_line[slot + at, pl.ds(within, rows), :].astype(F32)
            total = total + jnp.where(which == digit, own, found)
        target[pl.ds(within, rows), :] = total.astype(BF16)

    def give_home(number):
        section = PIECES[number][0]
        rows, at = part_of[number], piece_at[number]
        within = at // group
        for level in range(len(levels) - 1):
            add_level(number, level, k.line_sum.at[level + 1])
            send_level(number, level + 1)
        add_level(number, len(levels) - 1, k.home)
        target = k.got_all.at[pl.ds(section_at[number] + mine * rows, rows)]

        def give(other):
            remote(
                k.home.at[pl.ds(within, rows)],
                target,
                k.home_send.at[number],
                k.home_recv.at[number],
                {"phase": section, "batch": 2 * line + other},
            ).start()

        @pl.when(stage != section)
        def unused_both():
            give(0)
            give(1)

        @pl.when(stage == section)
        def unused_one():
            give(1 - core)
            target[...] = k.home[pl.ds(within, rows), :]

    def take_all(number):
        rows, within = part_of[number], section_at[number]

        @pl.when(stage == PIECES[number][0])
        def unused_take():
            wait_for(k.home_recv.at[number], k.got_all.at[pl.ds(within, (group - 1) * rows)])

    def end_sends(number):
        rows, at = part_of[number], piece_at[number]
        within = at // group
        wait_for(k.scatter_send.at[number], k.got_scatter.at[:, pl.ds(within, rows)])
        for level in range(len(levels)):
            size, unused_stride, slot, unused_digit = level_of(level)
            sent = k.got_line.at[pl.ds(slot, size - 1), pl.ds(within, rows)]
            wait_for(k.line_send.at[level, number], sent)

        @pl.when(stage != PIECES[number][0])
        def unused_away():
            wait_for(k.home_send.at[number], k.got_all.at[pl.ds(0, 2 * rows)])

        @pl.when(stage == PIECES[number][0])
        def unused_home():
            wait_for(k.home_send.at[number], k.got_all.at[pl.ds(0, rows)])

    def stage_piece(number):
        rows, used, at = padded[number], PIECES[number][1], piece_at[number]
        if used < rows:
            wst[used:rows, :] = jnp.zeros((rows - used, LANES), F32)

        def convert(i, carry):
            start = pl.multiple_of(i * 64, 64)
            k.gb[pl.ds(at + start, 64), :] = wst[pl.ds(start, 64), :].astype(BF16)
            return carry

        lax.fori_loop(0, rows // 64, convert, 0)
        give_scatter(number)

    def put_narrow(number, row, vector):
        k.send_narrow[number, row : row + 1, :] = vector

    def put_wide(number, row, vectors):
        for j, vector in enumerate(vectors):
            at = STARTS[number] + 4 * row + j
            k.send[at : at + 1, :] = vector

    def put_small(row, vector):
        k.small[row : row + 1, :] = vector

    def narrow(row):
        return k.total[row : row + 1, :]

    def wide(row):
        return jnp.concatenate([k.total[4 * row + j : 4 * row + j + 1, :] for j in range(4)], axis=1)

    def reduced(values):
        return jnp.sum(values, axis=0, keepdims=True)

    def gain_narrow(row):
        return k.gains[row : row + 1, :]

    def gain_wide(row):
        return jnp.concatenate([k.gains[row + j : row + j + 1, :] for j in range(4)], axis=1)

    def put_coef(layer, what, vector):
        row = 8 * layer + what
        k.coef[row : row + 1, 0 : vector.shape[1]] = vector

    def lanes(j):
        return slice(j * LANES, (j + 1) * LANES)

    def get_coef(layer, what, j=0):
        row = 8 * layer + what
        return k.coef[row : row + 1, lanes(j)]

    def finish(layer, sums, squares, gain, bias, count_inverse):
        mean = sums * count_inverse
        inverse = lax.rsqrt(squares * count_inverse - mean * mean + EPSILON)
        scale = inverse * gain
        put_coef(layer, INVERSE, inverse)
        put_coef(layer, NEG_MEAN, -mean * inverse)
        put_coef(layer, HALF_SCALE, 0.5 * scale)
        put_coef(layer, HALF_SHIFT, 0.5 * (bias - mean * scale))

    def normed_sum(layer, sums, products, j=0):
        return products * get_coef(layer, INVERSE, j) + sums * get_coef(layer, NEG_MEAN, j)

    def finish_back(layer, sums, dots, gain, count_inverse):
        width = sums.shape[1]
        row = 8 * layer
        inverse = k.coef[row + INVERSE : row + INVERSE + 1, 0:width]
        scale = inverse * gain
        slant = scale * dots * count_inverse
        put_coef(layer, GRAD_A, scale)
        put_coef(layer, GRAD_E, slant * inverse)
        put_coef(
            layer,
            GRAD_D,
            scale * sums * count_inverse
            + slant * k.coef[row + NEG_MEAN : row + NEG_MEAN + 1, 0:width],
        )

    def put_late(stores):
        for ref, at, value in stores:
            ref[at] = value

    def each_part(body, carry=0, parts=1):
        def step(i, inner):
            stores = []
            for u in range(parts):
                inner, found = body(pl.multiple_of((i * parts + u) * part, 16), inner)
                stores = stores + found
            put_late(stores)
            return inner

        return lax.fori_loop(0, 25 // parts, step, carry, unroll=UNROLL if parts == 1 else 1)

    def each_chunk(body, carry=0):
        def step(i, inner):
            return body(pl.multiple_of(i * chunk, 16), inner)

        return lax.fori_loop(0, 5, step, carry, unroll=UNROLL)

    def each_block(body):
        def step(i, carry):
            stores = []
            for u in range(per):
                number = i * per + u
                stores = stores + body(number, pl.multiple_of(number * BLOCK, 16))
            put_late(stores)
            return carry

        lax.fori_loop(0, blocks // per, step, 0, unroll=UNROLL)

    def zeros(width=MID):
        return jnp.zeros((8, width), F32)

    def live_rows(start, rows):
        return lax.broadcasted_iota(jnp.int32, (rows, LANES), 0) + start < rows_live

    def near_rows(rows, number):
        return lax.broadcasted_iota(jnp.int32, (rows, LANES), 0) < number

    def live_block(width):
        return jnp.broadcast_to(jnp.where(width > 0, 1.0, 0.0), (BLOCK, LANES)).astype(BF16)

    def at_block(buffer, j, start, rows):
        return buffer[pl.ds(j * out_rows + start, rows), :]

    def wide_store(buffer, start, values):
        rows = values.shape[0]
        for j in range(4):
            buffer[pl.ds(j * out_rows + start, rows), :] = values[:, lanes(j)]

    def added(carry, values):
        return carry[0] + folded(values), carry[1] + folded(values * values)

    def product_sums(left, right, store):
        width = right.shape[1]

        def body(start, carry):
            values = dense(left[pl.ds(start, chunk), :], right[...])
            store(start, values)
            return added(carry, values)

        return each_chunk(body, (zeros(width), zeros(width)))

    def store_narrow(target):
        def store(start, values):
            target[pl.ds(start, values.shape[0]), :] = values

        return store

    def send_narrow(number, sums):
        put_narrow(number, 0, reduced(sums[0]))
        put_narrow(number, 1, reduced(sums[1]))
        share(number)

    def by_lanes(vector):
        return [vector[:, lanes(j)] for j in range(4)]

    def stage_section(section):
        def step(i, carry):
            start = pl.multiple_of(i * (ROWS // 7), 16)
            wst[pl.ds(start, ROWS // 7), :] = wts[section, pl.ds(start, ROWS // 7), :].astype(F32)
            return carry

        lax.fori_loop(0, 7, step, 0)

    def unpack_wide(at, rows, target):
        for j in range(4):
            for r in range(rows // LANES):
                piece = wst[pl.ds(at + 4 * LANES * r + j, LANES, stride=4), :]
                target[r * LANES : (r + 1) * LANES, lanes(j)] = piece.astype(BF16)

    def take_gain(row, at, rows=1):
        k.gains[row : row + rows, :] = wst[at : at + rows, :]

    def turned(piece):
        return piece.astype(BF16).T

    tab_copy.wait()
    src[0:PAD, :] = jnp.zeros((PAD, LANES), F32)
    src[PAD + out_rows : plane, :] = jnp.zeros((PAD, LANES), F32)
    for number in range(4):
        big0[number * plane : number * plane + PAD, :] = jnp.zeros((PAD, LANES), F32)

    def make_masks(number, start):
        width, local = tab[0, number], tab[1, number]
        pixel = lax.broadcasted_iota(jnp.int32, (BLOCK, LANES), 0).astype(F32) + local.astype(F32)
        side = jnp.maximum(width, 1).astype(F32)
        row = jnp.floor((pixel + 0.5) / side)
        column = pixel - row * side
        one = jnp.where(width > 0, 1.0, 0.0)
        found = (row > 0.5, row < side - 1.5, column > 0.5, column < side - 1.5)
        return [
            (
                masks,
                (which, pl.ds(start, BLOCK), slice(None)),
                jnp.where(condition, one, 0.0).astype(BF16),
            )
            for which, condition in enumerate(found)
        ]

    each_block(make_masks)
    to_rows(EARLY, ROW)
    weight_copies = weight_copies + send_weights(1)
    for copy in feat_copies:
        copy.wait()

    window_rows = AHEAD + 4 * part

    def shortcut_pixels(i, carry):
        low = pl.multiple_of(jnp.maximum(i * 4 * part - AHEAD, 0), 16)
        stores = []
        for half in range(2):
            gn[half * window_rows : (half + 1) * window_rows, :] = feat[
                pl.ds(low, window_rows), lanes(half)
            ].astype(F32)
        for u in range(per):
            number = i * per + u
            start = pl.multiple_of(number * BLOCK, 16)
            first = tab[12, number]
            second = first + tab[4, number]
            near = near_rows(BLOCK, tab[3, number])
            one = jnp.where(tab[0, number] > 0, 1.0, 0.0)
            for half in range(2):
                picked = jnp.where(
                    near,
                    gn[pl.ds(half * window_rows + first, BLOCK, stride=2), :],
                    gn[pl.ds(half * window_rows + second, BLOCK, stride=2), :],
                )
                stores.append(
                    (k.xs, (pl.ds(start, BLOCK), lanes(half)), (picked * one).astype(BF16))
                )
        put_late(stores)
        return carry

    lax.fori_loop(0, 25, shortcut_pixels, 0)

    need_weights(0, 0)
    def open_first(step, carry):
        start = pl.multiple_of(step * chunk, 16)
        values = dense(feat[pl.ds(start, chunk), :], wts[0, 0:CIN, :])
        t1[pl.ds(start, chunk), :] = values
        rows = lax.broadcasted_iota(jnp.int32, values.shape, 0) + start
        return added(carry, jnp.where(rows < 4 * rows_live, values, 0.0))

    sums = lax.fori_loop(0, in_rows // chunk, open_first, (zeros(), zeros()), unroll=UNROLL)
    send_narrow(0, sums)

    need_weights(1, 0)
    stage_section(0)
    take_gain(0, IN_GAIN, 2)
    take_gain(2, MID_GAIN, 2)
    k.wmid1[...] = wst[MID_AT : MID_AT + 9 * MID, :].astype(BF16)

    def first_products(block):
        rows = slice(block * out_rows, (block + 1) * out_rows)
        live = (
            lax.broadcasted_iota(jnp.int32, (out_rows, MID), 0) + block * out_rows < 4 * rows_live
        )
        k.turn[0:LANES, :] = turned(jnp.where(live, t1[rows, :], 0.0))
        live = lax.broadcasted_iota(jnp.int32, (16, out_rows), 1) + block * out_rows < 4 * rows_live
        k.turn[LANES : LANES + 16, :] = jnp.where(live, 1.0, 0.0).astype(BF16)
        found = dense(k.turn[...], feat[rows, :])
        for half in range(2):
            at = slice(half * LANES, (half + 1) * LANES)
            product = found[0:LANES, lanes(half)].T
            total = jnp.broadcast_to(found[LANES : LANES + 1, lanes(half)], (LANES, LANES)).T
            k.first_t[at, :] = product if block == 0 else k.first_t[at, :] + product
            k.first_s[at, :] = total if block == 0 else k.first_s[at, :] + total

    first_products(0)
    collect(0)
    finish(L1, narrow(0), narrow(1), gain_narrow(0), gain_narrow(1), 0.25 * inverse_count)

    def first_hidden(number, start):
        scale, shift = get_coef(L1, HALF_SCALE), get_coef(L1, HALF_SHIFT)
        near = near_rows(BLOCK, tab[3, number])
        stores = []
        for row in range(2):
            for column in range(2):
                first = tab[2, number] + column + (tab[6, number] if row else 0)
                values = jnp.where(
                    near,
                    t1[pl.ds(first, BLOCK, stride=2), :],
                    t1[pl.ds(first + tab[4, number], BLOCK, stride=2), :],
                )
                at = pl.ds((2 * row + column) * plane + PAD + start, BLOCK)
                stores.append((big0, (at, slice(None)), silu_half(values * scale + shift)))
        return stores

    each_block(first_hidden)

    def wide_columns(number, start):
        width = tab[0, number]
        here = pl.ds(start, BLOCK)
        top, left, live = masks[0, here, :], masks[2, here, :], live_block(width)
        corner = top * left
        stores = []
        for tap in range(9):
            i, j = tap // 3, tap % 3
            at = (2 * (0 if i == 1 else 1) + (0 if j == 1 else 1)) * plane + PAD + start
            at = at - (width if i == 0 else 0) - (1 if j == 0 else 0)
            mask = (corner if j == 0 else top) if i == 0 else (left if j == 0 else live)
            values = big0[pl.ds(at, BLOCK), :].astype(BF16) * mask
            stores.append((k.cols1, (here, lanes(tap)), values))
        return stores

    each_block(wide_columns)
    send_narrow(1, product_sums(k.cols1, k.wmid1, store_narrow(k.t2)))

    bank_copies[0].start()
    need_weights(0, 1)
    need_weights(1, 1)
    stage_section(1)
    take_gain(8, OUT_GAIN, 8)
    take_gain(16, SHORT_GAIN, 8)
    unpack_wide(0, MID, k.wout2)
    unpack_wide(AFTER_OUT, CIN, k.wshort)
    short_sums = product_sums(k.xs, k.wshort, functools.partial(wide_store, big2))
    put_wide(2, 2, by_lanes(reduced(short_sums[0])))
    put_wide(2, 3, by_lanes(reduced(short_sums[1])))

    def close_narrow(layer, source, target):
        def body(start, carry):
            half = source[pl.ds(start, part), :] * get_coef(layer, HALF_SCALE) + get_coef(
                layer, HALF_SHIFT
            )
            values = jnp.where(live_rows(start, part), silu_half(half), 0.0).astype(BF16)
            return carry, [(target, (pl.ds(start, part), slice(None)), values)]

        each_part(body, parts=5)

    collect(1)
    finish(L2, narrow(0), narrow(1), gain_narrow(2), gain_narrow(3), inverse_count)
    close_narrow(L2, k.t2, k.h2)

    sums = product_sums(k.h2, k.wout2, functools.partial(wide_store, big1))
    put_wide(2, 0, by_lanes(reduced(sums[0])))
    put_wide(2, 1, by_lanes(reduced(sums[1])))
    share(2)

    def bank_to_bf16(half):
        bank_copies[half].wait()

        def body(i, carry):
            start = pl.multiple_of(i * 128, 128)
            for j in range(2):
                wide2[pl.ds(start, 128), lanes(2 * half + j)] = big0[
                    pl.ds(j * (BANK // 4) + start, 128), :
                ].astype(BF16)
            return carry

        lax.fori_loop(0, BANK // 4 // 128, body, 0)

    need_weights(0, 2)
    need_weights(1, 2)
    stage_section(2)
    take_gain(4, THIRD_GAIN, 2)
    take_gain(6, THIRD_MID_GAIN, 2)
    k.wmid3[...] = wst[THIRD_MID : THIRD_MID + 9 * MID, :].astype(BF16)
    bank_to_bf16(0)
    bank_copies[1].start()
    collect(2)
    finish(L3, wide(0), wide(1), gain_wide(8), gain_wide(12), inverse_count)
    finish(LS, wide(2), wide(3), gain_wide(16), gain_wide(20), inverse_count)

    def second_half(j, start):
        return (
            at_block(big1, j, start, part) * get_coef(L3, HALF_SCALE, j)
            + at_block(big2, j, start, part) * get_coef(LS, HALF_SCALE, j)
            + (get_coef(L3, HALF_SHIFT, j) + get_coef(LS, HALF_SHIFT, j))
        )

    def close_second(start, carry):
        live = live_rows(start, part)
        stores = []
        for j in range(4):
            values = jnp.where(live, silu_half(second_half(j, start)), 0.0).astype(BF16)
            stores.append((k.y, (pl.ds(start, part), lanes(j)), values))
        return carry, stores

    each_part(close_second)

    send_narrow(3, product_sums(k.y, wts.at[2, pl.ds(0, COUT)], store_narrow(k.t4)))
    need_weights(0, 3)
    need_weights(1, 3)
    stage_section(3)
    take_gain(24, OUT_GAIN, 8)
    unpack_wide(0, MID, k.wout4)
    bank_to_bf16(1)
    first_products(1)
    collect(3)
    finish(L4, narrow(0), narrow(1), gain_narrow(4), gain_narrow(5), inverse_count)

    def third_hidden(start, carry):
        half = k.t4[pl.ds(start, part), :] * get_coef(L4, HALF_SCALE) + get_coef(L4, HALF_SHIFT)
        return carry, [(src, (pl.ds(PAD + start, part), slice(None)), silu_half(half))]

    each_part(third_hidden, parts=5)

    def near_columns(number, start, target, target_start):
        width = tab[0, number]
        here = pl.ds(start, BLOCK)
        top, bottom, left, right = (masks[which, here, :] for which in range(4))
        live = live_block(width)
        stores = []
        for tap in range(9):
            i, j = tap // 3, tap % 3
            at = PAD + start + (i - 1) * width + (j - 1)
            mask = (top, live, bottom)[i]
            if j != 1:
                beside = left if j == 0 else right
                mask = beside if i == 1 else mask * beside
            values = src[pl.ds(at, BLOCK), :].astype(BF16) * mask
            stores.append((target, (pl.ds(target_start, BLOCK), lanes(tap)), values))
        return stores

    each_block(lambda number, start: near_columns(number, start, k.cols2, start))
    send_narrow(4, product_sums(k.cols2, k.wmid3, store_narrow(k.t5)))

    neg_copy.wait()
    gn[0 : 8 * LANES, :] = jnp.zeros((8 * LANES, LANES), F32)
    neg_piece = 512
    for slot in range(slots):

        def count(i, carry, slot=slot):
            at = pl.multiple_of(i * neg_piece, neg_piece)
            found = k.neg[slot, pl.ds(stage, 1), pl.ds(at, neg_piece)]
            spot = lax.broadcasted_iota(jnp.int32, (LANES, neg_piece), 0)
            upper = lax.shift_right_logical(found, 7)
            high = jnp.where(spot == upper, 1.0, 0.0).astype(BF16)
            low = jnp.where(spot == found - LANES * upper, 1.0, 0.0).astype(BF16)
            return carry + across(high, low)

        found = lax.fori_loop(
            0, NEG // neg_piece, count, jnp.zeros((LANES, LANES), F32), unroll=True
        )
        gn[pl.ds(slot, LANES, stride=8), :] = found
    collect(4)
    finish(L5, narrow(0), narrow(1), gain_narrow(6), gain_narrow(7), inverse_count)
    close_narrow(L5, k.t5, k.h4)

    sums = product_sums(k.h4, k.wout4, functools.partial(wide_store, big0))
    put_wide(5, 0, by_lanes(reduced(sums[0])))
    put_wide(5, 1, by_lanes(reduced(sums[1])))
    share(5)
    for j in range(4):
        k.wout4_t[j * LANES : (j + 1) * LANES, :] = turned(k.wout4[:, lanes(j)])
    for tap in range(9):
        k.wmid3_t[(8 - tap) * MID : (9 - tap) * MID, :] = turned(
            k.wmid3[tap * MID : (tap + 1) * MID, :]
        )
    for r in range(4):
        k.win3_t[:, lanes(r)] = turned(wts[2, r * LANES : (r + 1) * LANES, :])
    first_products(2)
    collect(5)
    finish(L6, wide(0), wide(1), gain_wide(24), gain_wide(28), inverse_count)

    def last_half(j, start):
        return (
            at_block(big0, j, start, part) * get_coef(L6, HALF_SCALE, j)
            + get_coef(L6, HALF_SHIFT, j)
            + 0.5 * k.y[pl.ds(start, part), lanes(j)].astype(F32)
        )

    def close_last(start, carry):
        return carry, [
            (gw, (pl.ds(start, part), lanes(j)), silu_half(last_half(j, start)).astype(BF16))
            for j in range(4)
        ]

    each_part(close_last)

    def pool(start, carry):
        rows = lax.broadcasted_iota(jnp.int32, (8, chunk), 1) + start
        owner = jnp.zeros((8, chunk), jnp.int32)
        for end in ends:
            owner = owner + jnp.where(rows >= end, 1, 0)
        mine = owner == lax.broadcasted_iota(jnp.int32, (8, chunk), 0)
        mine = jnp.where(mine, 1.0, 0.0).astype(BF16)
        return carry + dense(mine, gw[pl.ds(start, chunk), :])

    slot_row = lax.broadcasted_iota(jnp.int32, (8, LANES), 0)
    area = jnp.zeros((8, LANES), jnp.int32)
    positive = jnp.full((8, LANES), -1, jnp.int32)
    for slot in range(slots):
        area = jnp.where(slot_row == slot, sides[slot] * sides[slot], area)
        positive = jnp.where(slot_row == slot, k.positives[0, stage, slot], positive)
    inverse_area = jnp.where(area > 0, 1.0 / jnp.maximum(area, 1).astype(F32), 0.0)
    inverse_area_wide = jnp.concatenate([inverse_area] * 4, axis=1)
    half_offset = 0.5 * jnp.log(jnp.full((8, LANES), k.normalizer[0] * NEG / BANK))
    pooled = each_chunk(pool, zeros(COUT)) * inverse_area_wide

    head = wst[AFTER_OUT : AFTER_OUT + COUT, :].astype(BF16)
    pooled_high, pooled_low = split(pooled)
    embed = dense(pooled_high, head) + dense(pooled_low, head)
    scale = lax.rsqrt(jnp.sum(embed * embed, axis=1, keepdims=True) + 1e-06)
    unit = embed * scale
    unit_parts = jnp.concatenate(split(unit), axis=0)
    lane = lax.broadcasted_iota(jnp.int32, (8, LANES), 1)
    parts = []
    for block in range(4):
        scores = across(unit_parts, wide2[:, lanes(block)])
        scores = scores[0:8, :] + scores[8:16, :]
        pieces = []
        for j in range(BANK // 4 // LANES):
            high = block * (BANK // 4 // LANES) + j
            half = scores[:, lanes(j)] * (0.5 / SOFTMAX_TEMPER) - half_offset
            sigma = 0.5 + 0.5 * jnp.tanh(half)
            chosen = jnp.where(positive == lane + high * LANES, 1.0, 0.0)
            pieces.append((gn[high * 8 : high * 8 + 8, :] + chosen) * sigma - chosen)
        parts = parts + list(split(jnp.concatenate(pieces, axis=1)))
    found = dense(jnp.concatenate(parts, axis=0), wide2[...])
    unit_grad = zeros(EMB)
    for block in range(4):
        for row in (16 * block, 16 * block + 8):
            unit_grad = unit_grad + found[row : row + 8, lanes(block)]
    unit_grad = jnp.where(inverse_area > 0.0, unit_grad, 0.0) * (1.0 / SOFTMAX_TEMPER)
    embed_grad = scale * unit_grad - embed * (
        scale * scale * scale * jnp.sum(embed * unit_grad, axis=1, keepdims=True)
    )
    grad_high, grad_low = split(embed_grad)
    pooled_grad = across(grad_high, head) + across(grad_low, head)
    pooled_grad = pooled_grad * inverse_area_wide
    for j in range(4):
        k.spread[8 * j : 8 * j + 8, :] = pooled_grad[:, lanes(j)]

    def last_slope(step, carry):
        start = pl.multiple_of(step * part, 16)
        owners = [tab[5, step * per + u] for u in range(per)]
        found, stores = [], []
        for j in range(4):
            upstream = jnp.concatenate(
                [
                    jnp.broadcast_to(k.spread[pl.ds(8 * j + owner, 1), :], (BLOCK, LANES))
                    for owner in owners
                ],
                axis=0,
            )
            upstream = upstream * slope_half(last_half(j, start))
            stores.append((gw, (pl.ds(start, part), lanes(j)), upstream.astype(BF16)))
            found.append(
                (
                    carry[j][0] + folded(upstream),
                    carry[j][1] + folded(upstream * at_block(big0, j, start, part)),
                )
            )
        put_late(stores)
        return tuple(found)

    pair = (zeros(), zeros())
    sums = lax.fori_loop(0, 25, last_slope, (pair,) * 4, unroll=UNROLL)
    bias_grads = [reduced(sums[j][0]) for j in range(4)]
    gain_grads = [normed_sum(L6, bias_grads[j], reduced(sums[j][1]), j) for j in range(4)]
    put_wide(6, 0, bias_grads)
    put_wide(6, 1, gain_grads)
    share(6)
    for j in range(4):
        wst[OUT_GAIN + j : OUT_GAIN + j + 1, :] = gain_grads[j]
        wst[OUT_BIAS + j : OUT_BIAS + j + 1, :] = bias_grads[j]
    wst[AFTER_OUT : AFTER_OUT + COUT, :] = (
        outer(pooled_high, grad_high) + outer(pooled_high, grad_low) + outer(pooled_low, grad_high)
    )
    for j in range(4):
        k.wout2_t[j * LANES : (j + 1) * LANES, :] = turned(k.wout2[:, lanes(j)])
        for r in range(2):
            k.wshort_t[j * LANES : (j + 1) * LANES, lanes(r)] = turned(
                k.wshort[r * LANES : (r + 1) * LANES, lanes(j)]
            )
    def put_turned(source, target, values):
        at = (target // 2) * 4 * MID + source * MID
        k.wmid1_t[at : at + MID, lanes(target % 2)] = values

    for tap in range(9):
        i, j = tap // 3, tap % 3
        source = 2 * (1 if i == 0 else 0) + (1 if j == 0 else 0)
        target = 2 * (0 if i == 1 else 1) + (0 if j == 1 else 1)
        put_turned(source, target, turned(k.wmid1[tap * MID : (tap + 1) * MID, :]))
    for source in range(4):
        for target in range(4):
            if source & target != source:
                put_turned(source, target, jnp.zeros((MID, MID), BF16))
    first_products(3)
    collect(6)
    finish_back(L6, wide(0), wide(1), gain_wide(24), inverse_count)

    def back_value(layer, upstream, values, j=0):
        return (
            upstream * get_coef(layer, GRAD_A, j)
            - values * get_coef(layer, GRAD_E, j)
            - get_coef(layer, GRAD_D, j)
        )

    def back_sixth(start, carry):
        here = pl.ds(start, part)
        live = live_rows(start, part)
        stores = []
        for j in range(4):
            values = back_value(
                L6, gw[here, lanes(j)].astype(F32), at_block(big0, j, start, part), j
            )
            stores.append((wide2, (here, lanes(j)), jnp.where(live, values, 0.0).astype(BF16)))
        return carry, stores

    each_part(back_sixth)

    def back_narrow(layer, upstream, values, carry):
        half = values * get_coef(layer, HALF_SCALE) + get_coef(layer, HALF_SHIFT)
        upstream = upstream * slope_half(half)
        return upstream, (carry[0] + folded(upstream), carry[1] + folded(upstream * values))

    def back_rows(layer, values):
        def body(start, carry):
            here = pl.ds(start, part)
            upstream, carry = back_narrow(layer, gn[here, :], values[here, :], carry)
            return carry, [(gn, (here, slice(None)), upstream)]

        return each_part(body, (zeros(), zeros()), parts=5)

    def send_back(number, row, layer, sums):
        bias_grad = reduced(sums[0])
        gain_grad = normed_sum(layer, bias_grad, reduced(sums[1]))
        put_narrow(number, 0, bias_grad)
        put_narrow(number, 1, gain_grad)
        share(number)
        put_small(row, gain_grad)
        put_small(row + 1, bias_grad)

    def rounded_product(left, right):
        def body(start, carry):
            here = pl.ds(start, chunk)
            gn[here, :] = dense(left[here, :], right[...]).astype(BF16).astype(F32)
            return carry

        each_chunk(body)

    rounded_product(wide2, k.wout4_t)
    send_back(7, 2, L5, back_rows(L5, k.t5))

    def put_wide_matrix(at, values):
        for r in range(values.shape[0] // LANES):
            for j in range(4):
                wst[pl.ds(at + 4 * LANES * r + j, LANES, stride=4), :] = values[
                    r * LANES : (r + 1) * LANES, lanes(j)
                ]

    def turned_rows(ref, lane=0):
        return turned(ref[:, lane * LANES : (lane + 1) * LANES])

    k.turn[0:LANES, :] = turned_rows(k.h4)
    put_wide_matrix(0, dense(k.turn[0:LANES, :], wide2[0:out_rows, :]))
    stage_piece(LAST)
    collect(7)
    finish_back(L5, narrow(0), narrow(1), gain_narrow(6), inverse_count)

    def back_close(layer, values):
        def body(start, carry):
            here = pl.ds(start, part)
            found = back_value(layer, gn[here, :], values[here, :])
            found = jnp.where(live_rows(start, part), found, 0.0).astype(BF16)
            return carry, [
                (k.dtn, (here, slice(None)), found),
                (src, (pl.ds(PAD + start, part), slice(None)), found.astype(F32)),
            ]

        each_part(body, parts=5)

    back_close(L5, k.t5)

    def open_back_fourth(step, carry):
        chunk_start = pl.multiple_of(step * chunk, 16)

        def fill(i, inner):
            stores = []
            for u in range(per):
                at = pl.multiple_of((i * per + u) * BLOCK, 16)
                number = step * (chunk // BLOCK) + i * per + u
                stores = stores + near_columns(number, chunk_start + at, k.colt, at)
            put_late(stores)
            return inner

        lax.fori_loop(0, chunk // BLOCK // per, fill, 0, unroll=UNROLL)
        gn[pl.ds(chunk_start, chunk), :] = dense(k.colt[...], k.wmid3_t[...])
        return carry

    lax.fori_loop(0, 5, open_back_fourth, 0)
    send_back(8, 0, L4, back_rows(L4, k.t4))

    def columns_grad(columns, store):
        k.turn[0:LANES, :] = turned_rows(k.dtn)
        for group in range(3):
            found = dense(k.turn[0:LANES, :], columns[:, 3 * group * LANES : 3 * (group + 1) * LANES])
            for j in range(3):
                store(3 * group + j, found[:, lanes(j)].T)

    def store_third(tap, values):
        wst[THIRD_MID + tap * MID : THIRD_MID + (tap + 1) * MID, :] = values

    columns_grad(k.cols2, store_third)
    give_line(LAST)
    collect(8)
    finish_back(L4, narrow(0), narrow(1), gain_narrow(4), inverse_count)
    back_close(L4, k.t4)

    def back_block(start, carry):
        here = pl.ds(start, part)
        arrived = dense(k.dtn[here, :], k.win3_t[...])
        found, stores = [], []
        for j in range(4):
            upstream = arrived[:, lanes(j)] + gw[here, lanes(j)].astype(F32)
            upstream = upstream.astype(BF16).astype(F32) * slope_half(second_half(j, start))
            stores.append((gw, (here, lanes(j)), upstream.astype(BF16)))
            found.append(
                (
                    carry[j][0] + folded(upstream),
                    carry[j][1] + folded(upstream * at_block(big1, j, start, part)),
                    carry[j][2] + folded(upstream * at_block(big2, j, start, part)),
                )
            )
        return tuple(found), stores

    sums = each_part(back_block, ((zeros(), zeros(), zeros()),) * 4)
    bias_grads, gain_grads, short_grads = (
        [reduced(sums[j][which]) for j in range(4)] for which in range(3)
    )
    gain_grads = [normed_sum(L3, bias_grads[j], gain_grads[j], j) for j in range(4)]
    short_grads = [normed_sum(LS, bias_grads[j], short_grads[j], j) for j in range(4)]
    put_wide(9, 0, bias_grads)
    put_wide(9, 1, gain_grads)
    put_wide(9, 2, short_grads)
    share(9)
    k.turn[0:LANES, :] = turned_rows(k.dtn)
    found = dense(k.turn[0:LANES, :], k.y[...])
    for j in range(4):
        wst[j * LANES : (j + 1) * LANES, :] = found[:, lanes(j)].T
    wst[THIRD_GAIN : THIRD_BIAS + 1, :] = k.small[0:2, :]
    wst[THIRD_MID_GAIN : THIRD_MID_BIAS + 1, :] = k.small[2:4, :]
    stage_piece(THIRD)
    give_home(LAST)
    collect(9)
    finish_back(L3, wide(0), wide(1), gain_wide(8), inverse_count)
    finish_back(LS, wide(0), wide(2), gain_wide(16), inverse_count)

    def back_third(start, carry):
        here = pl.ds(start, part)
        below = pl.ds(out_rows + start, part)
        live = live_rows(start, part)
        stores = []
        for j in range(4):
            upstream = gw[here, lanes(j)].astype(F32)
            found = back_value(L3, upstream, at_block(big1, j, start, part), j)
            stores.append((wide2, (here, lanes(j)), jnp.where(live, found, 0.0).astype(BF16)))
            found = back_value(LS, upstream, at_block(big2, j, start, part), j)
            stores.append((wide2, (below, lanes(j)), jnp.where(live, found, 0.0).astype(BF16)))
        return carry, stores

    each_part(back_third)
    rounded_product(wide2, k.wout2_t)
    send_back(10, 6, L2, back_rows(L2, k.t2))
    for j in range(4):
        wst[OUT_GAIN + j : OUT_GAIN + j + 1, :] = gain_grads[j]
        wst[OUT_BIAS + j : OUT_BIAS + j + 1, :] = bias_grads[j]
        wst[SHORT_GAIN + j : SHORT_GAIN + j + 1, :] = short_grads[j]
        wst[SHORT_BIAS + j : SHORT_BIAS + j + 1, :] = bias_grads[j]
    k.turn[0:LANES, :] = turned_rows(k.h2)
    put_wide_matrix(0, dense(k.turn[0:LANES, :], wide2[0:out_rows, :]))
    for half in range(2):
        k.turn[0:LANES, :] = turned_rows(k.xs, half)
        put_wide_matrix(
            AFTER_OUT + half * 4 * LANES, dense(k.turn[0:LANES, :], wide2[out_rows : 2 * out_rows, :])
        )
    stage_piece(SECOND)
    give_line(THIRD)

    def back_picked(start, carry):
        found = dense(wide2[pl.ds(out_rows + start, chunk), :], k.wshort_t[...])
        found = found.astype(BF16).astype(F32)
        for half in range(2):
            big2[pl.ds(half * plane + PAD + start, chunk), :] = found[:, lanes(half)]
        return carry

    each_chunk(back_picked)
    for half in range(2):
        big2[half * plane : half * plane + PAD, :] = jnp.zeros((PAD, LANES), F32)
    collect(10)
    finish_back(L2, narrow(0), narrow(1), gain_narrow(2), inverse_count)
    back_close(L2, k.t2)


    def back_planes(step, carry):
        chunk_start = pl.multiple_of(step * chunk, 16)

        def fill(i, inner):
            stores = []
            for u in range(per):
                at = pl.multiple_of((i * per + u) * BLOCK, 16)
                start = chunk_start + at
                here = pl.ds(start, BLOCK)
                width = tab[0, step * (chunk // BLOCK) + i * per + u]
                bottom, right, live = masks[1, here, :], masks[3, here, :], live_block(width)
                shifts = ((0, live), (1, right), (width, bottom), (width + 1, bottom * right))
                for number, (shift, mask) in enumerate(shifts):
                    values = src[pl.ds(PAD + start + shift, BLOCK), :].astype(BF16) * mask
                    stores.append((k.colt, (pl.ds(at, BLOCK), lanes(number)), values))
            put_late(stores)
            return inner

        lax.fori_loop(0, chunk // BLOCK // per, fill, 0, unroll=UNROLL)
        even = dense(k.colt[:, 0 : 2 * MID], k.wmid1_t[0 : 2 * MID, :])
        odd = dense(k.colt[:, 0 : 4 * MID], k.wmid1_t[4 * MID : 8 * MID, :])
        for number in range(4):
            found = (even, odd)[number // 2][:, lanes(number % 2)]
            big0[pl.ds(number * plane + PAD + chunk_start, chunk), :] = found
        return carry

    lax.fori_loop(0, 5, back_planes, 0)

    in_unroll = 10

    def back_first(i, carry):
        stores = []
        for u in range(in_unroll):
            number = i * in_unroll + u
            first, second = tab[7, number], tab[8, number]
            near = near_rows(8, tab[9, number])
            for column in range(2):
                at = pl.ds(number * BLOCK + column, 8, stride=2)
                hidden = jnp.where(
                    near,
                    big0[pl.ds(first + column * plane, 8), :],
                    big0[pl.ds(second + column * plane, 8), :],
                )
                upstream, carry = back_narrow(L1, hidden, t1[at, :], carry)
                stores.append((big1, (at, slice(None)), upstream))
        put_late(stores)
        return carry

    sums = lax.fori_loop(
        0, in_rows // BLOCK // in_unroll, back_first, (zeros(), zeros()), unroll=UNROLL
    )
    send_back(11, 4, L1, sums)
    def store_first(tap, values):
        at = piece_at[FIRST_MID] + tap * MID
        k.gb[at : at + MID, :] = values.astype(BF16)

    columns_grad(k.cols1, store_first)
    if padded[FIRST_MID] > 9 * MID:
        at = piece_at[FIRST_MID]
        k.gb[at + 9 * MID : at + padded[FIRST_MID], :] = jnp.zeros(
            (padded[FIRST_MID] - 9 * MID, LANES), BF16
        )
    give_scatter(FIRST_MID)
    give_line(SECOND)
    give_home(THIRD)

    found = jnp.zeros((MID, CIN), F32)
    for block in range(4):
        rows = slice(block * out_rows, (block + 1) * out_rows)
        k.turn[0:LANES, :] = turned(big1[rows, :])
        found = found + dense(k.turn[0:LANES, :], feat[rows, :])
    first_g = [found[:, lanes(half)].T for half in range(2)]
    gn[0 : 2 * window_rows, :] = jnp.zeros((2 * window_rows, LANES), F32)
    for half in range(2):
        k.win1_t[:, lanes(half)] = turned(wts[0, half * LANES : (half + 1) * LANES, :])
    collect(11)
    finish_back(L1, narrow(0), narrow(1), gain_narrow(0), 0.25 * inverse_count)

    at = piece_at[FIRST_IN]
    for half in range(2):
        rows = slice(half * LANES, (half + 1) * LANES)
        values = first_g[half] * get_coef(L1, GRAD_A) - k.first_t[rows, :] * get_coef(L1, GRAD_E)
        values = values - k.first_s[rows, :] * get_coef(L1, GRAD_D)
        k.gb[at + half * LANES : at + (half + 1) * LANES, :] = values.astype(BF16)
    k.gb[at + CIN : at + CIN + 16, :] = jnp.concatenate(
        [k.small[4:8, :], jnp.zeros((12, LANES), F32)], axis=0
    ).astype(BF16)
    k.gb[at + CIN + 16 : at + padded[FIRST_IN], :] = jnp.zeros(
        (padded[FIRST_IN] - CIN - 16, LANES), BF16
    )
    give_scatter(FIRST_IN)
    give_line(FIRST_MID)
    give_home(SECOND)

    for block in range(4):

        def close_back_first(start, carry, block=block):
            rows = pl.ds(block * out_rows + start, part)
            found = back_value(L1, big1[rows, :], t1[rows, :])
            row = lax.broadcasted_iota(jnp.int32, (part, MID), 0) + (block * out_rows + start)
            found = jnp.where(row < 4 * rows_live, found, 0.0).astype(BF16)
            return carry, [(gw, (pl.ds(start, part), lanes(block)), found)]

        each_part(close_back_first, parts=5)

    give_line(FIRST_IN)
    give_home(FIRST_MID)

    def input_grad(step, carry):
        block, start = lax.div(step, 5), pl.multiple_of(lax.rem(step, 5) * chunk, 16)
        stores = []
        for u in range(chunk // BLOCK):
            number = step * (chunk // BLOCK) + u
            near = near_rows(8, tab[9, number])
            for half in range(2):
                values = jnp.where(
                    near,
                    big2[pl.ds(tab[10, number] + half * plane, 8), :],
                    big2[pl.ds(tab[11, number] + half * plane, 8), :],
                )
                at = slice(half * window_rows + u * BLOCK, half * window_rows + (u + 1) * BLOCK, 2)
                stores.append((gn, (at, slice(None)), values))
        put_late(stores)
        lane = pl.ds(pl.multiple_of(block * LANES, LANES), LANES)
        found = dense(gw[pl.ds(start, chunk), lane], k.win1_t[...])
        rows = pl.ds(pl.multiple_of(step * chunk, 16), chunk)
        for half in range(2):
            feat[rows, lanes(half)] = (
                found[:, lanes(half)] + gn[half * window_rows : half * window_rows + chunk, :]
            ).astype(BF16)
        return carry

    lax.fori_loop(0, 10, input_grad, 0)
    give_home(FIRST_IN)
    lax.fori_loop(10, 20, input_grad, 0)
    input_copy = pltpu.make_async_copy(feat, k.input_grad_at, k.out_sem.at[0])
    input_copy.start()

    for number in range(len(PIECES)):
        take_all(number)

    def ordered(target, source, rows):
        def body(i, carry):
            start = pl.multiple_of(i * 32, 32)
            wst[pl.ds(target + start, 32), :] = k.got_all[pl.ds(source + start, 32), :].astype(F32)
            return carry

        lax.fori_loop(0, rows // 32, body, 0)

    def blank(at):
        wst[at:ROWS, :] = jnp.zeros((ROWS - at, LANES), F32)

    for number in (LAST, THIRD, SECOND):

        @pl.when(stage == PIECES[number][0])
        def unused_ordered(number=number):
            rows = min(padded[number], ROWS // 32 * 32)
            if rows < ROWS:
                blank(rows)
            ordered(0, 0, rows)
            if rows < PIECES[number][1]:
                tail = k.got_all[rows : rows + 16, :].astype(F32)
                wst[rows : rows + 16, :] = tail

    @pl.when(stage == 0)
    def unused_first():
        at = section_at[FIRST_IN]
        blank(MID_BIAS + 1)
        ordered(0, at, CIN)
        gains = k.got_all[at + CIN : at + CIN + 16, :].astype(F32)
        wst[IN_GAIN : IN_BIAS + 1, :] = gains[0:2, :]
        wst[MID_GAIN : MID_BIAS + 1, :] = gains[2:4, :]
        ordered(MID_AT, 0, 9 * MID)

    out_copy = pltpu.make_async_copy(wst.at[pl.ds(0, ROWS)], k.weight_grads_at, k.grad_sem)
    out_copy.start()
    input_copy.wait()
    for copy in weight_copies:
        copy.wait_send()
    for number in range(EXCHANGES):
        wait_for(k.stat_send.at[number], incoming(number, pl.ds(0, batches - 1)))
    for number in range(len(PIECES)):
        end_sends(number)
    out_copy.wait()


def write_kernel(weight_rows, input_rows, weight_out, input_out):
    input_out[...] = input_rows[...]

    @pl.when(pl.program_id(0) == 0)
    def unused_weights():
        weight_out.reshape(ROW, LANES)[...] = weight_rows[0:ROW, :]


def shards(features, weights, crop_kind, positives, negatives, bank, normalizer):
    phases = lax.axis_size("phase")
    batches = lax.axis_size("batch")
    in_rows = features.shape[0] // MICRO
    out_rows = in_rows // 4
    plane = out_rows + 2 * PAD
    slots = crop_kind.shape[2]
    chunk = out_rows // 5
    part = out_rows // 25
    group = 2 * phases
    levels = line_levels(batches // 2)
    padded = [-(-rows // (16 * group)) * 16 * group for unused, rows in PIECES]
    widest = max(*padded[:3], padded[3] + padded[4])
    eighth = sum(padded) // group
    staged = max(ROWS, *padded[:3])
    any_space = pl.BlockSpec(memory_space=pl.ANY)
    smem = pl.BlockSpec(memory_space=pltpu.SMEM)

    def held(*shape, dtype=F32):
        return pltpu.VMEM(shape, dtype)

    def sems(*shape):
        return pltpu.SemaphoreType.DMA(shape)

    def low(*shape):
        return held(*shape, dtype=BF16)

    inputs = {
        "features_at": (features, any_space),
        "weights_at": (weights, any_space),
        "negatives_at": (jnp.transpose(negatives, (0, 2, 1, 3)), any_space),
        "bank_at": (bank, any_space),
        "kinds": (jnp.transpose(crop_kind, (2, 1, 0)), smem),
        "positives": (positives, smem),
        "normalizer": (normalizer, smem),
    }
    outputs = {
        "weight_grads_at": jax.ShapeDtypeStruct((ROWS, LANES), F32),
        "input_grad_at": jax.ShapeDtypeStruct((in_rows, CIN), BF16),
    }
    scratch = {
        "feat": low(in_rows, CIN),
        "t1": held(in_rows, MID),
        "big0": held(4 * plane, MID),
        "big1": held(in_rows, MID),
        "big2": held(4 * plane, MID),
        "cols1": low(out_rows, 9 * MID),
        "cols2": low(out_rows, 9 * MID),
        "colt": low(chunk, 9 * MID),
        "src": held(plane, MID),
        "t2": held(out_rows, MID),
        "t4": held(out_rows, MID),
        "t5": held(out_rows, MID),
        "gn": held(out_rows, MID),
        "h2": low(out_rows, MID),
        "h4": low(out_rows, MID),
        "xs": low(out_rows, CIN),
        "y": low(out_rows, COUT),
        "gw": low(out_rows, COUT),
        "wide2": low(BANK // 4, COUT),
        "dtn": low(out_rows, MID),
        "turn": low(LANES + 16, out_rows),
        "first_t": held(CIN, MID),
        "first_s": held(CIN, MID),
        "masks": low(4, out_rows, LANES),
        "raw": low(1, GRAD_LEN),
        "wts": low(phases, ROWS, LANES),
        "wst": held(staged, LANES),
        "wmid1": low(9 * MID, MID),
        "wmid3": low(9 * MID, MID),
        "wout2": low(MID, COUT),
        "wshort": low(CIN, COUT),
        "wout4": low(MID, COUT),
        "wout2_t": low(COUT, MID),
        "wshort_t": low(COUT, CIN),
        "wout4_t": low(COUT, MID),
        "wmid1_t": low(8 * MID, 2 * MID),
        "wmid3_t": low(9 * MID, MID),
        "win1_t": low(MID, CIN),
        "win3_t": low(MID, COUT),
        "gains": held(32, LANES),
        "small": held(8, LANES),
        "coef": held(56, COUT),
        "spread": held(32, LANES),
        "neg": held(slots, MICRO, NEG, dtype=jnp.int32),
        "tabv": held(16, TABLE, dtype=jnp.int32),
        "tab": pltpu.SMEM((16, TABLE), jnp.int32),
        "send": held(SPAN_ROWS, LANES),
        "send_narrow": held(EXCHANGES, 2, LANES),
        "recv_narrow": held(EXCHANGES, batches, 2, LANES),
        "recv": held(batches, SPAN_ROWS, LANES),
        "total": held(16, LANES),
        "gb": low(sum(padded), LANES),
        "got_scatter": low(group - 1, eighth, LANES),
        "line_sum": low(len(levels), eighth, LANES),
        "got_line": low(sum(levels) - len(levels), eighth, LANES),
        "home": low(eighth, LANES),
        "got_all": low(widest, LANES),
        "raw_sem": pltpu.SemaphoreType.DMA,
        "feat_sem": sems(4),
        "bank_sem": sems(2),
        "neg_sem": pltpu.SemaphoreType.DMA,
        "tab_sem": pltpu.SemaphoreType.DMA,
        "weight_send": sems(2, phases),
        "weight_recv": sems(2, phases),
        "stat_send": sems(EXCHANGES),
        "stat_recv": sems(EXCHANGES),
        "scatter_send": sems(len(PIECES)),
        "scatter_recv": sems(len(PIECES)),
        "line_send": sems(len(levels), len(PIECES)),
        "line_recv": sems(len(levels), len(PIECES)),
        "home_send": sems(len(PIECES)),
        "home_recv": sems(len(PIECES)),
        "out_sem": sems(4),
        "grad_sem": pltpu.SemaphoreType.DMA,
    }
    names = (*inputs, *outputs, *scratch)
    weight_rows, input_rows = pl.pallas_call(
        functools.partial(kernel, names, batches, phases, in_rows, slots),
        out_shape=tuple(outputs.values()),
        in_specs=[spec for unused, spec in inputs.values()],
        out_specs=(any_space, any_space),
        scratch_shapes=list(scratch.values()),
        compiler_params=pltpu.CompilerParams(
            collective_id=0, has_side_effects=True, vmem_limit_bytes=64 * 1024 * 1024
        ),
    )(*[value for value, unused in inputs.values()])
    steps = 4
    rows = pl.BlockSpec((in_rows // steps, CIN), lambda i: (i, 0))
    weight_grads, input_grad = pl.pallas_call(
        write_kernel,
        grid=(steps,),
        out_shape=(
            jax.ShapeDtypeStruct((1, GRAD_LEN), F32),
            jax.ShapeDtypeStruct((in_rows, CIN), BF16),
        ),
        in_specs=[pl.BlockSpec((ROWS, LANES), lambda i: (0, 0)), rows],
        out_specs=(pl.BlockSpec((1, GRAD_LEN), lambda i: (0, 0)), rows),
        compiler_params=pltpu.CompilerParams(vmem_limit_bytes=64 * 1024 * 1024),
    )(weight_rows, input_rows)
    return (weight_grads, input_grad)


def solution(mesh):
    placed = (
        P("batch", None),
        P("phase", None),
        P(),
        P("batch", None, None),
        P("batch", None, None, None),
        P(),
        P(),
    )
    return jax.shard_map(
        shards,
        mesh=mesh,
        in_specs=placed,
        out_specs=(P("phase", None), P(("batch", "phase"), None)),
        check_vma=False,
    )
```

time: 5230 us -> 129 us (0.02)
  other arithmetic: 1750 us -> 0 us
  local copies, waits for them, and re-layouts: 1590 us -> 0 us
  waiting for transfers between devices: 790 us -> 0 us
  blocking collectives: 399 us -> 0 us
  loops' own time: 396 us -> 0 us
  matrix products: 220 us -> 0 us
  Pallas kernels: 0 us -> 127 us
    scatter-add x21 -> x0, other arithmetic: 1040 us -> none  [the longest x7 817 us: scatter_taps(): jax.ops.segment_sum(spread.reshape(-1, channels), index.reshape(-1), num_...]
    gather x21 -> x0, local copies, waits for them, and re-layouts: 779 us -> none  [gather_taps(): jnp.take(source, index.reshape(-1), axis=0)]
    ppermute x14 -> x0, waiting for transfers between devices: 643 us -> none  [shifted(): return lax.ppermute(block, axis, route)]
    reshape x72 -> x0, local copies, waits for them, and re-layouts: 441 us -> none  [the longest x42 344 us: gather_taps(): jnp.take(source, index.reshape(-1), axis=0)]
    psum x28 -> x0, blocking collectives: 399 us -> none  [the longest x14 200 us: norm_back_totals(): return lax.psum(local, 'batch')]
    another operation x44 -> x0, loops' own time: 396 us -> none  [the longest x7 171 us: backward_step(): lax.switch(phase, backward_open, arriving, kept, stats, micro, backward_b...]
    select_n x112 -> x0, other arithmetic: 315 us -> none  [the longest x42 271 us: gather_taps(): jnp.take(source, index.reshape(-1), axis=0)]
    dot_general x56 -> x0, matrix products: 220 us -> none  [the longest x42 186 us: dense(): return jnp.dot(left, right, preferred_element_type=jnp.float32)]
  transfers between devices with their start and end apart: 16 -> 0, of which waited for: 16 -> 0; matrix products, arithmetic and copies ran while one was open for 3% -> 0% of each run, Pallas kernels for 0% -> 0%
where the time goes in v1:
time: 129 us; the launch traced here: 128 us
  Pallas kernels  127 us (98%)
  between operations  1.29 us (1%)
    pallas_call x1, Pallas kernels, shards(): pl.pallas_call(functools.partial(kernel, names, batches, phases, in_rows,...  122 us
    pallas_call x1, Pallas kernels, shards(): pl.pallas_call(write_kernel, grid=(steps,), out_shape=(jax.ShapeDtypeStru...  5.27 us

profile of v1, /device:TPU:0, one launch (start us, length us, event | category | flops | bytes accessed | tf_op | source)
XLA Modules:
  0.0 128.4 jit_solution(3178372940490064948)
XLA Ops:
  1.3 121.8 %shard_map.86 = (f32[1680,128]{1,0:T(8,128)}, bf16[8000,256]{1,0:T(8,128)(2,1)}) custom-call(bf16[32000,256]{1,0:T(8,128)(2,1)} %refs_0_.1, bf16[1,213504]{1,0:T(2,128)(2,1)} %refs_1_.1, s32[1,5,4,4096]{3,2,1,0:T(4,128)} %bitcast.2, f32[16384,128]{1,0:T(8,128)} %refs_3_.1, s32[5,4,8]{2,1,0:T(4,128)} %bitcast.3, s32[1,4,5]{2,1,0:T(4,128)} %refs_5_.1, ...), custom_call_target="tpu_custom_call" | custom-call | tf_op jit(solution)/shard_map/pallas_call | solution.py:1571
  123.1 5.3 %shard_map.87 = (f32[1,213504]{1,0:T(1,128)}, bf16[8000,256]{1,0:T(8,128)(2,1)}) custom-call(f32[1680,128]{1,0:T(8,128)} %get-tuple-element.4.weight_rows, bf16[8000,256]{1,0:T(8,128)(2,1)} %get-tuple-element.5.input_rows), custom_call_target="tpu_custom_call" | custom-call | tf_op jit(solution)/shard_map/pallas_call | solution.py:1583

commit v2 on v1

--- a/solution.py
+++ b/solution.py
@@ -235,6 +235,7 @@
     even_below = jnp.where(in_live & (in_left < 8) & (odd == 1), PAD + below, 0)
     columns = (width, local, begin, left, jump, slot, 2 * width)
     columns = columns + (at_here, at_below, in_left, even_here, even_below, in_window)
+    k.tabv[...] = jnp.zeros(k.tabv.shape, jnp.int32)
     for number, column in enumerate(columns):
         k.tabv[number : number + 1, :] = column
     tab_copy = pltpu.make_async_copy(k.tabv, tab, k.tab_sem)
@@ -312,11 +313,16 @@
                 incoming(number, me),
                 k.stat_send.at[number],
                 k.stat_recv.at[number],
-                batch_peer(i),
+                {"batch": lax.rem(batches - 1 - me + i, batches)},
             ).start()
             return carry
 
-        lax.fori_loop(1, batches, give, 0, unroll=batches <= 8)
+        mirrored = lax.rem(2 * me + 1, batches)
+
+        def skip(i, carry):
+            return give(i + jnp.where(i >= mirrored, 1, 0), carry)
+
+        lax.fori_loop(0, batches - 1, skip, 0, unroll=batches <= 8)
         incoming(number, me)[...] = outgoing(number)[...]
 
     def collect(number):
@@ -602,12 +608,14 @@
     def added(carry, values):
         return carry[0] + folded(values), carry[1] + folded(values * values)
 
-    def product_sums(left, right, store):
+    def product_sums(left, right, store, masked=False):
         width = right.shape[1]
 
         def body(start, carry):
             values = dense(left[pl.ds(start, chunk), :], right[...])
             store(start, values)
+            if masked:
+                values = jnp.where(live_rows(start, chunk), values, 0.0)
             return added(carry, values)
 
         return each_chunk(body, (zeros(width), zeros(width)))
@@ -804,6 +812,51 @@
     finish(L2, narrow(0), narrow(1), gain_narrow(2), gain_narrow(3), inverse_count)
     close_narrow(L2, k.t2, k.h2)
 
+    roomy = hasattr(k, "slope23")
+
+    def worked_slope(layer, values):
+        return slope_half(values * get_coef(layer, HALF_SCALE) + get_coef(layer, HALF_SHIFT))
+
+    def keep_narrow_slope(layer, source, target):
+        def body(start, carry):
+            here = pl.ds(start, part)
+            values = worked_slope(layer, source[here, :]).astype(BF16)
+            return carry, [(target, (here, slice(None)), values)]
+
+        each_part(body, parts=5)
+
+    def second_slope(j, start):
+        if roomy:
+            return k.slope23[pl.ds(start, part), lanes(j)].astype(F32)
+        return slope_half(second_half(j, start))
+
+    def keep_second_slope():
+        def body(start, carry):
+            return carry, [
+                (
+                    k.slope23,
+                    (pl.ds(start, part), lanes(j)),
+                    slope_half(second_half(j, start)).astype(BF16),
+                )
+                for j in range(4)
+            ]
+
+        if roomy:
+            each_part(body)
+
+    def keep_first_slope():
+        def body(start, carry):
+            return carry, [
+                (
+                    k.cols2,
+                    (pl.ds(start, part), lanes(block)),
+                    worked_slope(L1, t1[pl.ds(block * out_rows + start, part), :]).astype(BF16),
+                )
+                for block in range(4)
+            ]
+
+        each_part(body)
+
     sums = product_sums(k.h2, k.wout2, functools.partial(wide_store, big1))
     put_wide(2, 0, by_lanes(reduced(sums[0])))
     put_wide(2, 1, by_lanes(reduced(sums[1])))
@@ -842,16 +895,15 @@
         )
 
     def close_second(start, carry):
-        live = live_rows(start, part)
         stores = []
         for j in range(4):
-            values = jnp.where(live, silu_half(second_half(j, start)), 0.0).astype(BF16)
+            values = silu_half(second_half(j, start)).astype(BF16)
             stores.append((k.y, (pl.ds(start, part), lanes(j)), values))
         return carry, stores
 
     each_part(close_second)
 
-    send_narrow(3, product_sums(k.y, wts.at[2, pl.ds(0, COUT)], store_narrow(k.t4)))
+    send_narrow(3, product_sums(k.y, wts.at[2, pl.ds(0, COUT)], store_narrow(k.t4), True))
     need_weights(0, 3)
     need_weights(1, 3)
     stage_section(3)
@@ -859,6 +911,7 @@
     unpack_wide(0, MID, k.wout4)
     bank_to_bf16(1)
     first_products(1)
+    keep_second_slope()
     collect(3)
     finish(L4, narrow(0), narrow(1), gain_narrow(4), gain_narrow(5), inverse_count)
 
@@ -923,6 +976,7 @@
     for r in range(4):
         k.win3_t[:, lanes(r)] = turned(wts[2, r * LANES : (r + 1) * LANES, :])
     first_products(2)
+    keep_narrow_slope(L5, k.t5, k.dtn)
     collect(5)
     finish(L6, wide(0), wide(1), gain_wide(24), gain_wide(28), inverse_count)
 
@@ -1063,26 +1117,22 @@
 
     def back_sixth(start, carry):
         here = pl.ds(start, part)
-        live = live_rows(start, part)
         stores = []
         for j in range(4):
             values = back_value(
                 L6, gw[here, lanes(j)].astype(F32), at_block(big0, j, start, part), j
             )
-            stores.append((wide2, (here, lanes(j)), jnp.where(live, values, 0.0).astype(BF16)))
+            stores.append((wide2, (here, lanes(j)), values.astype(BF16)))
         return carry, stores
 
     each_part(back_sixth)
 
-    def back_narrow(layer, upstream, values, carry):
-        half = values * get_coef(layer, HALF_SCALE) + get_coef(layer, HALF_SHIFT)
-        upstream = upstream * slope_half(half)
-        return upstream, (carry[0] + folded(upstream), carry[1] + folded(upstream * values))
-
-    def back_rows(layer, values):
+    def back_rows(values, slope):
         def body(start, carry):
             here = pl.ds(start, part)
-            upstream, carry = back_narrow(layer, gn[here, :], values[here, :], carry)
+            upstream = gn[here, :] * slope[here, :].astype(F32)
+            upstream = jnp.where(live_rows(start, part), upstream, 0.0)
+            carry = (carry[0] + folded(upstream), carry[1] + folded(upstream * values[here, :]))
             return carry, [(gn, (here, slice(None)), upstream)]
 
         return each_part(body, (zeros(), zeros()), parts=5)
@@ -1105,7 +1155,7 @@
         each_chunk(body)
 
     rounded_product(wide2, k.wout4_t)
-    send_back(7, 2, L5, back_rows(L5, k.t5))
+    send_back(7, 2, L5, back_rows(k.t5, k.dtn))
 
     def put_wide_matrix(at, values):
         for r in range(values.shape[0] // LANES):
@@ -1120,6 +1170,7 @@
     k.turn[0:LANES, :] = turned_rows(k.h4)
     put_wide_matrix(0, dense(k.turn[0:LANES, :], wide2[0:out_rows, :]))
     stage_piece(LAST)
+    keep_narrow_slope(L4, k.t4, k.h4)
     collect(7)
     finish_back(L5, narrow(0), narrow(1), gain_narrow(6), inverse_count)
 
@@ -1153,8 +1204,8 @@
         gn[pl.ds(chunk_start, chunk), :] = dense(k.colt[...], k.wmid3_t[...])
         return carry
 
-    lax.fori_loop(0, 5, open_back_fourth, 0)
-    send_back(8, 0, L4, back_rows(L4, k.t4))
+    lax.fori_loop(0, 5, open_back_fourth, 0, unroll=UNROLL)
+    send_back(8, 0, L4, back_rows(k.t4, k.h4))
 
     def columns_grad(columns, store):
         k.turn[0:LANES, :] = turned_rows(k.dtn)
@@ -1168,6 +1219,7 @@
 
     columns_grad(k.cols2, store_third)
     give_line(LAST)
+    keep_narrow_slope(L2, k.t2, k.h4)
     collect(8)
     finish_back(L4, narrow(0), narrow(1), gain_narrow(4), inverse_count)
     back_close(L4, k.t4)
@@ -1178,7 +1230,7 @@
         found, stores = [], []
         for j in range(4):
             upstream = arrived[:, lanes(j)] + gw[here, lanes(j)].astype(F32)
-            upstream = upstream.astype(BF16).astype(F32) * slope_half(second_half(j, start))
+            upstream = upstream.astype(BF16).astype(F32) * second_slope(j, start)
             stores.append((gw, (here, lanes(j)), upstream.astype(BF16)))
             found.append(
                 (
@@ -1207,6 +1259,7 @@
     wst[THIRD_MID_GAIN : THIRD_MID_BIAS + 1, :] = k.small[2:4, :]
     stage_piece(THIRD)
     give_home(LAST)
+    keep_first_slope()
     collect(9)
     finish_back(L3, wide(0), wide(1), gain_wide(8), inverse_count)
     finish_back(LS, wide(0), wide(2), gain_wide(16), inverse_count)
@@ -1214,19 +1267,18 @@
     def back_third(start, carry):
         here = pl.ds(start, part)
         below = pl.ds(out_rows + start, part)
-        live = live_rows(start, part)
         stores = []
         for j in range(4):
             upstream = gw[here, lanes(j)].astype(F32)
             found = back_value(L3, upstream, at_block(big1, j, start, part), j)
-            stores.append((wide2, (here, lanes(j)), jnp.where(live, found, 0.0).astype(BF16)))
+            stores.append((wide2, (here, lanes(j)), found.astype(BF16)))
             found = back_value(LS, upstream, at_block(big2, j, start, part), j)
-            stores.append((wide2, (below, lanes(j)), jnp.where(live, found, 0.0).astype(BF16)))
+            stores.append((wide2, (below, lanes(j)), found.astype(BF16)))
         return carry, stores
 
     each_part(back_third)
     rounded_product(wide2, k.wout2_t)
-    send_back(10, 6, L2, back_rows(L2, k.t2))
+    send_back(10, 6, L2, back_rows(k.t2, k.h4))
     for j in range(4):
         wst[OUT_GAIN + j : OUT_GAIN + j + 1, :] = gain_grads[j]
         wst[OUT_BIAS + j : OUT_BIAS + j + 1, :] = bias_grads[j]
@@ -1257,57 +1309,64 @@
     back_close(L2, k.t2)
 
 
-    def back_planes(step, carry):
-        chunk_start = pl.multiple_of(step * chunk, 16)
-
-        def fill(i, inner):
-            stores = []
-            for u in range(per):
-                at = pl.multiple_of((i * per + u) * BLOCK, 16)
-                start = chunk_start + at
-                here = pl.ds(start, BLOCK)
-                width = tab[0, step * (chunk // BLOCK) + i * per + u]
-                bottom, right, live = masks[1, here, :], masks[3, here, :], live_block(width)
-                shifts = ((0, live), (1, right), (width, bottom), (width + 1, bottom * right))
-                for number, (shift, mask) in enumerate(shifts):
-                    values = src[pl.ds(PAD + start + shift, BLOCK), :].astype(BF16) * mask
-                    stores.append((k.colt, (pl.ds(at, BLOCK), lanes(number)), values))
-            put_late(stores)
-            return inner
-
-        lax.fori_loop(0, chunk // BLOCK // per, fill, 0, unroll=UNROLL)
-        even = dense(k.colt[:, 0 : 2 * MID], k.wmid1_t[0 : 2 * MID, :])
-        odd = dense(k.colt[:, 0 : 4 * MID], k.wmid1_t[4 * MID : 8 * MID, :])
+    def back_columns(number, start):
+        here = pl.ds(start, BLOCK)
+        width = tab[0, number]
+        bottom, right, live = masks[1, here, :], masks[3, here, :], live_block(width)
+        shifts = ((0, live), (1, right), (width, bottom), (width + 1, bottom * right))
+        return [
+            (
+                wide2,
+                (here, lanes(which)),
+                src[pl.ds(PAD + start + shift, BLOCK), :].astype(BF16) * mask,
+            )
+            for which, (shift, mask) in enumerate(shifts)
+        ]
+
+    each_block(back_columns)
+
+    def back_planes(start, carry):
+        here = pl.ds(start, chunk)
+        even = dense(wide2[here, 0 : 2 * MID], k.wmid1_t[0 : 2 * MID, :])
+        odd = dense(wide2[here, :], k.wmid1_t[4 * MID : 8 * MID, :])
         for number in range(4):
             found = (even, odd)[number // 2][:, lanes(number % 2)]
-            big0[pl.ds(number * plane + PAD + chunk_start, chunk), :] = found
+            big0[pl.ds(number * plane + PAD + start, chunk), :] = found
         return carry
 
-    lax.fori_loop(0, 5, back_planes, 0)
+    each_chunk(back_planes)
 
     in_unroll = 10
 
-    def back_first(i, carry):
+    def to_input_order(i, carry):
         stores = []
         for u in range(in_unroll):
             number = i * in_unroll + u
             first, second = tab[7, number], tab[8, number]
             near = near_rows(8, tab[9, number])
             for column in range(2):
-                at = pl.ds(number * BLOCK + column, 8, stride=2)
-                hidden = jnp.where(
+                values = jnp.where(
                     near,
                     big0[pl.ds(first + column * plane, 8), :],
                     big0[pl.ds(second + column * plane, 8), :],
                 )
-                upstream, carry = back_narrow(L1, hidden, t1[at, :], carry)
-                stores.append((big1, (at, slice(None)), upstream))
+                at = pl.ds(number * BLOCK + column, 8, stride=2)
+                stores.append((big1, (at, slice(None)), values))
         put_late(stores)
         return carry
 
-    sums = lax.fori_loop(
-        0, in_rows // BLOCK // in_unroll, back_first, (zeros(), zeros()), unroll=UNROLL
-    )
+    lax.fori_loop(0, in_rows // BLOCK // in_unroll, to_input_order, 0, unroll=UNROLL)
+
+    def back_first(start, carry):
+        stores = []
+        for block in range(4):
+            rows = pl.ds(block * out_rows + start, part)
+            upstream = big1[rows, :] * k.cols2[pl.ds(start, part), lanes(block)].astype(F32)
+            carry = (carry[0] + folded(upstream), carry[1] + folded(upstream * t1[rows, :]))
+            stores.append((big1, (rows, slice(None)), upstream))
+        return carry, stores
+
+    sums = each_part(back_first, (zeros(), zeros()))
     send_back(11, 4, L1, sums)
     def store_first(tap, values):
         at = piece_at[FIRST_MID] + tap * MID
@@ -1329,9 +1388,9 @@
         k.turn[0:LANES, :] = turned(big1[rows, :])
         found = found + dense(k.turn[0:LANES, :], feat[rows, :])
     first_g = [found[:, lanes(half)].T for half in range(2)]
-    gn[0 : 2 * window_rows, :] = jnp.zeros((2 * window_rows, LANES), F32)
     for half in range(2):
         k.win1_t[:, lanes(half)] = turned(wts[0, half * LANES : (half + 1) * LANES, :])
+    gn[...] = jnp.zeros(gn.shape, F32)
     collect(11)
     finish_back(L1, narrow(0), narrow(1), gain_narrow(0), 0.25 * inverse_count)
 
@@ -1365,33 +1424,36 @@
     give_line(FIRST_IN)
     give_home(FIRST_MID)
 
-    def input_grad(step, carry):
-        block, start = lax.div(step, 5), pl.multiple_of(lax.rem(step, 5) * chunk, 16)
-        stores = []
-        for u in range(chunk // BLOCK):
-            number = step * (chunk // BLOCK) + u
-            near = near_rows(8, tab[9, number])
+
+    def input_grad(block, carry):
+        lane = pl.ds(pl.multiple_of(block * LANES, LANES), LANES)
+        for piece in range(5):
+            low = (piece % 2) * 2 * chunk
+            stores = []
+            for u in range(chunk // BLOCK):
+                number = (block * 5 + piece) * (chunk // BLOCK) + u
+                near = near_rows(8, tab[9, number])
+                for half in range(2):
+                    values = jnp.where(
+                        near,
+                        big2[pl.ds(tab[10, number] + half * plane, 8), :],
+                        big2[pl.ds(tab[11, number] + half * plane, 8), :],
+                    )
+                    at = low + half * chunk + u * BLOCK
+                    stores.append((gn, (slice(at, at + BLOCK, 2), slice(None)), values))
+            put_late(stores)
+            found = dense(gw[piece * chunk : (piece + 1) * chunk, lane], k.win1_t[...])
+            rows = pl.ds(pl.multiple_of(block * out_rows + piece * chunk, 16), chunk)
             for half in range(2):
-                values = jnp.where(
-                    near,
-                    big2[pl.ds(tab[10, number] + half * plane, 8), :],
-                    big2[pl.ds(tab[11, number] + half * plane, 8), :],
+                at = low + half * chunk
+                feat[rows, lanes(half)] = (found[:, lanes(half)] + gn[at : at + chunk, :]).astype(
+                    BF16
                 )
-                at = slice(half * window_rows + u * BLOCK, half * window_rows + (u + 1) * BLOCK, 2)
-                stores.append((gn, (at, slice(None)), values))
-        put_late(stores)
-        lane = pl.ds(pl.multiple_of(block * LANES, LANES), LANES)
-        found = dense(gw[pl.ds(start, chunk), lane], k.win1_t[...])
-        rows = pl.ds(pl.multiple_of(step * chunk, 16), chunk)
-        for half in range(2):
-            feat[rows, lanes(half)] = (
-                found[:, lanes(half)] + gn[half * window_rows : half * window_rows + chunk, :]
-            ).astype(BF16)
         return carry
 
-    lax.fori_loop(0, 10, input_grad, 0)
+    lax.fori_loop(0, 2, input_grad, 0)
     give_home(FIRST_IN)
-    lax.fori_loop(10, 20, input_grad, 0)
+    lax.fori_loop(2, 4, input_grad, 0)
     input_copy = pltpu.make_async_copy(feat, k.input_grad_at, k.out_sem.at[0])
     input_copy.start()
 
@@ -1443,12 +1505,31 @@
     out_copy.wait()
 
 
-def write_kernel(weight_rows, input_rows, weight_out, input_out):
-    input_out[...] = input_rows[...]
-
-    @pl.when(pl.program_id(0) == 0)
-    def unused_weights():
-        weight_out.reshape(ROW, LANES)[...] = weight_rows[0:ROW, :]
+def write_kernel(weight_rows, input_rows, weight_out, input_out, held_weights, held, sems):
+    count = 10
+    part = input_rows.shape[0] // count
+    pairs = [
+        (weight_rows.at[pl.ds(0, ROW)], held_weights, weight_out.reshape(ROW, LANES)),
+        *[
+            (input_rows.at[rows], held.at[rows], input_out.at[rows])
+            for rows in [pl.ds(i * part, part) for i in range(count)]
+        ],
+    ]
+    arriving = [
+        pltpu.make_async_copy(source, middle, sems.at[0, i])
+        for i, (source, middle, target) in enumerate(pairs)
+    ]
+    leaving = [
+        pltpu.make_async_copy(middle, target, sems.at[1, i])
+        for i, (source, middle, target) in enumerate(pairs)
+    ]
+    for copy in arriving:
+        copy.start()
+    for i in range(len(pairs)):
+        arriving[i].wait()
+        leaving[i].start()
+    for copy in leaving:
+        copy.wait()
 
 
 def shards(features, weights, crop_kind, positives, negatives, bank, normalizer):
@@ -1477,6 +1558,8 @@
 
     def low(*shape):
         return held(*shape, dtype=BF16)
+
+    kept_slopes = {"slope23": low(out_rows, COUT)} if batches <= 8 else {}
 
     inputs = {
         "features_at": (features, any_space),
@@ -1536,6 +1619,7 @@
         "coef": held(56, COUT),
         "spread": held(32, LANES),
         "neg": held(slots, MICRO, NEG, dtype=jnp.int32),
+        **kept_slopes,
         "tabv": held(16, TABLE, dtype=jnp.int32),
         "tab": pltpu.SMEM((16, TABLE), jnp.int32),
         "send": held(SPAN_ROWS, LANES),
@@ -1572,23 +1656,21 @@
         functools.partial(kernel, names, batches, phases, in_rows, slots),
         out_shape=tuple(outputs.values()),
         in_specs=[spec for unused, spec in inputs.values()],
-        out_specs=(any_space, any_space),
+        out_specs=(any_space,) * len(outputs),
         scratch_shapes=list(scratch.values()),
         compiler_params=pltpu.CompilerParams(
             collective_id=0, has_side_effects=True, vmem_limit_bytes=64 * 1024 * 1024
         ),
     )(*[value for value, unused in inputs.values()])
-    steps = 4
-    rows = pl.BlockSpec((in_rows // steps, CIN), lambda i: (i, 0))
     weight_grads, input_grad = pl.pallas_call(
         write_kernel,
-        grid=(steps,),
         out_shape=(
             jax.ShapeDtypeStruct((1, GRAD_LEN), F32),
             jax.ShapeDtypeStruct((in_rows, CIN), BF16),
         ),
-        in_specs=[pl.BlockSpec((ROWS, LANES), lambda i: (0, 0)), rows],
-        out_specs=(pl.BlockSpec((1, GRAD_LEN), lambda i: (0, 0)), rows),
+        in_specs=[any_space, any_space],
+        out_specs=(any_space, any_space),
+        scratch_shapes=[held(ROW, LANES), low(in_rows, CIN), sems(2, 11)],
         compiler_params=pltpu.CompilerParams(vmem_limit_bytes=64 * 1024 * 1024),
     )(weight_rows, input_rows)
     return (weight_grads, input_grad)

time: 129 us -> 126 us (0.977)
  Pallas kernels: 127 us -> 124 us
    pallas_call x1, Pallas kernels: 122 us -> 120 us  [shards(): pl.pallas_call(functools.partial(kernel, names, batches, phases, in_rows,...]
where the time goes in v2:
time: 126 us
  Pallas kernels  124 us (98%)
  between operations  1.47 us (1%)
    pallas_call x1, Pallas kernels, shards(): pl.pallas_call(functools.partial(kernel, names, batches, phases, in_rows,...  120 us
    pallas_call x1, Pallas kernels, shards(): pl.pallas_call(write_kernel, out_shape=(jax.ShapeDtypeStruct((1, GRAD_LEN...  4.1 us

profile of v2, /device:TPU:0, one launch (start us, length us, event | category | flops | bytes accessed | tf_op | source)
XLA Modules:
  0.0 125.6 jit_solution(9263678042294878653)
XLA Ops:
  1.3 120.0 %shard_map.86 = (f32[1680,128]{1,0:T(8,128)}, bf16[8000,256]{1,0:T(8,128)(2,1)}) custom-call(bf16[32000,256]{1,0:T(8,128)(2,1)} %refs_0_.1, bf16[1,213504]{1,0:T(2,128)(2,1)} %refs_1_.1, s32[1,5,4,4096]{3,2,1,0:T(4,128)} %bitcast.2, f32[16384,128]{1,0:T(8,128)} %refs_3_.1, s32[5,4,8]{2,1,0:T(4,128)} %bitcast.3, s32[1,4,5]{2,1,0:T(4,128)} %refs_5_.1, ...), custom_call_target="tpu_custom_call" | custom-call | tf_op jit(solution)/shard_map/pallas_call | solution.py:1655
  121.3 4.1 %shard_map.87 = (f32[1,213504]{1,0:T(1,128)}, bf16[8000,256]{1,0:T(8,128)(2,1)}) custom-call(f32[1680,128]{1,0:T(8,128)} %get-tuple-element.4.weight_rows, bf16[8000,256]{1,0:T(8,128)(2,1)} %get-tuple-element.5.input_rows), custom_call_target="tpu_custom_call" | custom-call | tf_op jit(solution)/shard_map/pallas_call | solution.py:1665

commit v3 on v2

--- a/solution.py
+++ b/solution.py
@@ -486,7 +486,7 @@
             k.gb[pl.ds(at + start, 64), :] = wst[pl.ds(start, 64), :].astype(BF16)
             return carry
 
-        lax.fori_loop(0, rows // 64, convert, 0)
+        lax.fori_loop(0, rows // 64, convert, 0, unroll=2)
         give_scatter(number)
 
     def put_narrow(number, row, vector):
@@ -653,6 +653,22 @@
 
     def turned(piece):
         return piece.astype(BF16).T
+
+    to_rows(EARLY, ROW)
+    weight_copies = weight_copies + send_weights(1)
+    for copy in feat_copies:
+        copy.wait()
+
+    need_weights(0, 0)
+    def open_first(step, carry):
+        start = pl.multiple_of(step * chunk, 16)
+        values = dense(feat[pl.ds(start, chunk), :], wts[0, 0:CIN, :])
+        t1[pl.ds(start, chunk), :] = values
+        rows = lax.broadcasted_iota(jnp.int32, values.shape, 0) + start
+        return added(carry, jnp.where(rows < 4 * rows_live, values, 0.0))
+
+    sums = lax.fori_loop(0, in_rows // chunk, open_first, (zeros(), zeros()), unroll=UNROLL)
+    send_narrow(0, sums)
 
     tab_copy.wait()
     src[0:PAD, :] = jnp.zeros((PAD, LANES), F32)
@@ -678,51 +694,39 @@
         ]
 
     each_block(make_masks)
-    to_rows(EARLY, ROW)
-    weight_copies = weight_copies + send_weights(1)
-    for copy in feat_copies:
-        copy.wait()
-
     window_rows = AHEAD + 4 * part
 
     def shortcut_pixels(i, carry):
-        low = pl.multiple_of(jnp.maximum(i * 4 * part - AHEAD, 0), 16)
-        stores = []
-        for half in range(2):
-            gn[half * window_rows : (half + 1) * window_rows, :] = feat[
-                pl.ds(low, window_rows), lanes(half)
-            ].astype(F32)
-        for u in range(per):
-            number = i * per + u
-            start = pl.multiple_of(number * BLOCK, 16)
-            first = tab[12, number]
-            second = first + tab[4, number]
-            near = near_rows(BLOCK, tab[3, number])
-            one = jnp.where(tab[0, number] > 0, 1.0, 0.0)
+        for piece in range(5):
+            step = i * 5 + piece
+            at = (piece % 2) * 2 * window_rows
+            low = pl.multiple_of(jnp.maximum(step * 4 * part - AHEAD, 0), 16)
             for half in range(2):
-                picked = jnp.where(
-                    near,
-                    gn[pl.ds(half * window_rows + first, BLOCK, stride=2), :],
-                    gn[pl.ds(half * window_rows + second, BLOCK, stride=2), :],
-                )
-                stores.append(
-                    (k.xs, (pl.ds(start, BLOCK), lanes(half)), (picked * one).astype(BF16))
-                )
-        put_late(stores)
+                gn[at + half * window_rows : at + (half + 1) * window_rows, :] = feat[
+                    pl.ds(low, window_rows), lanes(half)
+                ].astype(F32)
+            stores = []
+            for u in range(per):
+                number = step * per + u
+                start = pl.multiple_of(number * BLOCK, 16)
+                first = tab[12, number]
+                second = first + tab[4, number]
+                near = near_rows(BLOCK, tab[3, number])
+                one = jnp.where(tab[0, number] > 0, 1.0, 0.0)
+                for half in range(2):
+                    base = at + half * window_rows
+                    picked = jnp.where(
+                        near,
+                        gn[pl.ds(base + first, BLOCK, stride=2), :],
+                        gn[pl.ds(base + second, BLOCK, stride=2), :],
+                    )
+                    stores.append(
+                        (k.xs, (pl.ds(start, BLOCK), lanes(half)), (picked * one).astype(BF16))
+                    )
+            put_late(stores)
         return carry
 
-    lax.fori_loop(0, 25, shortcut_pixels, 0)
-
-    need_weights(0, 0)
-    def open_first(step, carry):
-        start = pl.multiple_of(step * chunk, 16)
-        values = dense(feat[pl.ds(start, chunk), :], wts[0, 0:CIN, :])
-        t1[pl.ds(start, chunk), :] = values
-        rows = lax.broadcasted_iota(jnp.int32, values.shape, 0) + start
-        return added(carry, jnp.where(rows < 4 * rows_live, values, 0.0))
-
-    sums = lax.fori_loop(0, in_rows // chunk, open_first, (zeros(), zeros()), unroll=UNROLL)
-    send_narrow(0, sums)
+    lax.fori_loop(0, 5, shortcut_pixels, 0)
 
     need_weights(1, 0)
     stage_section(0)
@@ -746,7 +750,6 @@
             k.first_t[at, :] = product if block == 0 else k.first_t[at, :] + product
             k.first_s[at, :] = total if block == 0 else k.first_s[at, :] + total
 
-    first_products(0)
     collect(0)
     finish(L1, narrow(0), narrow(1), gain_narrow(0), gain_narrow(1), 0.25 * inverse_count)
 
@@ -808,6 +811,7 @@
 
         each_part(body, parts=5)
 
+    first_products(0)
     collect(1)
     finish(L2, narrow(0), narrow(1), gain_narrow(2), gain_narrow(3), inverse_count)
     close_narrow(L2, k.t2, k.h2)
@@ -873,7 +877,7 @@
                 ].astype(BF16)
             return carry
 
-        lax.fori_loop(0, BANK // 4 // 128, body, 0)
+        lax.fori_loop(0, BANK // 4 // 128, body, 0, unroll=4)
 
     need_weights(0, 2)
     need_weights(1, 2)
@@ -883,6 +887,7 @@
     k.wmid3[...] = wst[THIRD_MID : THIRD_MID + 9 * MID, :].astype(BF16)
     bank_to_bf16(0)
     bank_copies[1].start()
+    first_products(1)
     collect(2)
     finish(L3, wide(0), wide(1), gain_wide(8), gain_wide(12), inverse_count)
     finish(LS, wide(2), wide(3), gain_wide(16), gain_wide(20), inverse_count)
@@ -910,7 +915,6 @@
     take_gain(24, OUT_GAIN, 8)
     unpack_wide(0, MID, k.wout4)
     bank_to_bf16(1)
-    first_products(1)
     keep_second_slope()
     collect(3)
     finish(L4, narrow(0), narrow(1), gain_narrow(4), gain_narrow(5), inverse_count)
@@ -959,6 +963,7 @@
             0, NEG // neg_piece, count, jnp.zeros((LANES, LANES), F32), unroll=True
         )
         gn[pl.ds(slot, LANES, stride=8), :] = found
+    first_products(2)
     collect(4)
     finish(L5, narrow(0), narrow(1), gain_narrow(6), gain_narrow(7), inverse_count)
     close_narrow(L5, k.t5, k.h4)
@@ -975,8 +980,8 @@
         )
     for r in range(4):
         k.win3_t[:, lanes(r)] = turned(wts[2, r * LANES : (r + 1) * LANES, :])
-    first_products(2)
     keep_narrow_slope(L5, k.t5, k.dtn)
+    first_products(3)
     collect(5)
     finish(L6, wide(0), wide(1), gain_wide(24), gain_wide(28), inverse_count)
 
@@ -1104,7 +1109,6 @@
         for target in range(4):
             if source & target != source:
                 put_turned(source, target, jnp.zeros((MID, MID), BF16))
-    first_products(3)
     collect(6)
     finish_back(L6, wide(0), wide(1), gain_wide(24), inverse_count)
 
@@ -1424,6 +1428,17 @@
     give_line(FIRST_IN)
     give_home(FIRST_MID)
 
+
+    def ordered(target, source, rows):
+        def body(i, carry):
+            start = pl.multiple_of(i * 64, 64)
+            wst[pl.ds(target + start, 64), :] = k.got_all[pl.ds(source + start, 64), :].astype(F32)
+            return carry
+
+        lax.fori_loop(0, rows // 64, body, 0, unroll=2)
+
+    def blank(at):
+        wst[at:ROWS, :] = jnp.zeros((ROWS - at, LANES), F32)
 
     def input_grad(block, carry):
         lane = pl.ds(pl.multiple_of(block * LANES, LANES), LANES)
@@ -1453,29 +1468,25 @@
 
     lax.fori_loop(0, 2, input_grad, 0)
     give_home(FIRST_IN)
+    take_all(FIRST_MID)
+
+    @pl.when(stage == 0)
+    def unused_first_mid():
+        blank(MID_BIAS + 1)
+        ordered(MID_AT, 0, 9 * MID)
+
     lax.fori_loop(2, 4, input_grad, 0)
     input_copy = pltpu.make_async_copy(feat, k.input_grad_at, k.out_sem.at[0])
     input_copy.start()
 
-    for number in range(len(PIECES)):
+    for number in (LAST, THIRD, SECOND, FIRST_IN):
         take_all(number)
-
-    def ordered(target, source, rows):
-        def body(i, carry):
-            start = pl.multiple_of(i * 32, 32)
-            wst[pl.ds(target + start, 32), :] = k.got_all[pl.ds(source + start, 32), :].astype(F32)
-            return carry
-
-        lax.fori_loop(0, rows // 32, body, 0)
-
-    def blank(at):
-        wst[at:ROWS, :] = jnp.zeros((ROWS - at, LANES), F32)
 
     for number in (LAST, THIRD, SECOND):
 
         @pl.when(stage == PIECES[number][0])
         def unused_ordered(number=number):
-            rows = min(padded[number], ROWS // 32 * 32)
+            rows = min(padded[number], ROWS // 128 * 128)
             if rows < ROWS:
                 blank(rows)
             ordered(0, 0, rows)
@@ -1486,12 +1497,10 @@
     @pl.when(stage == 0)
     def unused_first():
         at = section_at[FIRST_IN]
-        blank(MID_BIAS + 1)
         ordered(0, at, CIN)
         gains = k.got_all[at + CIN : at + CIN + 16, :].astype(F32)
         wst[IN_GAIN : IN_BIAS + 1, :] = gains[0:2, :]
         wst[MID_GAIN : MID_BIAS + 1, :] = gains[2:4, :]
-        ordered(MID_AT, 0, 9 * MID)
 
     out_copy = pltpu.make_async_copy(wst.at[pl.ds(0, ROWS)], k.weight_grads_at, k.grad_sem)
     out_copy.start()

time: 126 us -> 125 us (level)
  no operation moved by 1% of the time
where the time goes in v3:
time: 125 us
  Pallas kernels  123 us (98%)
  between operations  1.47 us (1%)
    pallas_call x1, Pallas kernels, shards(): pl.pallas_call(functools.partial(kernel, names, batches, phases, in_rows,...  119 us
    pallas_call x1, Pallas kernels, shards(): pl.pallas_call(write_kernel, out_shape=(jax.ShapeDtypeStruct((1, GRAD_LEN...  4.1 us

profile of v3, /device:TPU:0, one launch (start us, length us, event | category | flops | bytes accessed | tf_op | source)
XLA Modules:
  0.0 124.8 jit_solution(9123998136846398296)
XLA Ops:
  1.3 119.3 %shard_map.86 = (f32[1680,128]{1,0:T(8,128)}, bf16[8000,256]{1,0:T(8,128)(2,1)}) custom-call(bf16[32000,256]{1,0:T(8,128)(2,1)} %refs_0_.1, bf16[1,213504]{1,0:T(2,128)(2,1)} %refs_1_.1, s32[1,5,4,4096]{3,2,1,0:T(4,128)} %bitcast.2, f32[16384,128]{1,0:T(8,128)} %refs_3_.1, s32[5,4,8]{2,1,0:T(4,128)} %bitcast.3, s32[1,4,5]{2,1,0:T(4,128)} %refs_5_.1, ...), custom_call_target="tpu_custom_call" | custom-call | tf_op jit(solution)/shard_map/pallas_call | solution.py:1664
  120.6 4.1 %shard_map.87 = (f32[1,213504]{1,0:T(1,128)}, bf16[8000,256]{1,0:T(8,128)(2,1)}) custom-call(f32[1680,128]{1,0:T(8,128)} %get-tuple-element.4.weight_rows, bf16[8000,256]{1,0:T(8,128)(2,1)} %get-tuple-element.5.input_rows), custom_call_target="tpu_custom_call" | custom-call | tf_op jit(solution)/shard_map/pallas_call | solution.py:1674

commit v4 on v3

--- a/solution.py
+++ b/solution.py
@@ -566,7 +566,7 @@
             put_late(stores)
             return inner
 
-        return lax.fori_loop(0, 25 // parts, step, carry, unroll=UNROLL if parts == 1 else 1)
+        return lax.fori_loop(0, 25 // parts, step, carry)
 
     def each_chunk(body, carry=0):
         def step(i, inner):
@@ -1078,7 +1078,7 @@
         return tuple(found)
 
     pair = (zeros(), zeros())
-    sums = lax.fori_loop(0, 25, last_slope, (pair,) * 4, unroll=UNROLL)
+    sums = lax.fori_loop(0, 25, last_slope, (pair,) * 4)
     bias_grads = [reduced(sums[j][0]) for j in range(4)]
     gain_grads = [normed_sum(L6, bias_grads[j], reduced(sums[j][1]), j) for j in range(4)]
     put_wide(6, 0, bias_grads)
@@ -1298,16 +1298,6 @@
     stage_piece(SECOND)
     give_line(THIRD)
 
-    def back_picked(start, carry):
-        found = dense(wide2[pl.ds(out_rows + start, chunk), :], k.wshort_t[...])
-        found = found.astype(BF16).astype(F32)
-        for half in range(2):
-            big2[pl.ds(half * plane + PAD + start, chunk), :] = found[:, lanes(half)]
-        return carry
-
-    each_chunk(back_picked)
-    for half in range(2):
-        big2[half * plane : half * plane + PAD, :] = jnp.zeros((PAD, LANES), F32)
     collect(10)
     finish_back(L2, narrow(0), narrow(1), gain_narrow(2), inverse_count)
     back_close(L2, k.t2)
@@ -1425,6 +1415,16 @@
 
         each_part(close_back_first, parts=5)
 
+    def back_picked(start, carry):
+        found = dense(wide2[pl.ds(out_rows + start, chunk), :], k.wshort_t[...])
+        found = found.astype(BF16).astype(F32)
+        for half in range(2):
+            big2[pl.ds(half * plane + PAD + start, chunk), :] = found[:, lanes(half)]
+        return carry
+
+    each_chunk(back_picked)
+    for half in range(2):
+        big2[half * plane : half * plane + PAD, :] = jnp.zeros((PAD, LANES), F32)
     give_line(FIRST_IN)
     give_home(FIRST_MID)
 

time: 125 us -> 130 us (1.040)
  Pallas kernels: 123 us -> 128 us
    pallas_call x1, Pallas kernels: 119 us -> 124 us  [shards(): pl.pallas_call(functools.partial(kernel, names, batches, phases, in_rows,...]
where the time goes in v4:
time: 130 us; the launch traced here: 129 us
  Pallas kernels  128 us (98%)
  between operations  1.47 us (1%)
    pallas_call x1, Pallas kernels, shards(): pl.pallas_call(functools.partial(kernel, names, batches, phases, in_rows,...  124 us
    pallas_call x1, Pallas kernels, shards(): pl.pallas_call(write_kernel, out_shape=(jax.ShapeDtypeStruct((1, GRAD_LEN...  4.1 us

profile of v4, /device:TPU:0, one launch (start us, length us, event | category | flops | bytes accessed | tf_op | source)
XLA Modules:
  0.0 129.3 jit_solution(7092371954661867627)
XLA Ops:
  1.3 123.8 %shard_map.86 = (f32[1680,128]{1,0:T(8,128)}, bf16[8000,256]{1,0:T(8,128)(2,1)}) custom-call(bf16[32000,256]{1,0:T(8,128)(2,1)} %refs_0_.1, bf16[1,213504]{1,0:T(2,128)(2,1)} %refs_1_.1, s32[1,5,4,4096]{3,2,1,0:T(4,128)} %bitcast.2, f32[16384,128]{1,0:T(8,128)} %refs_3_.1, s32[5,4,8]{2,1,0:T(4,128)} %bitcast.3, s32[1,4,5]{2,1,0:T(4,128)} %refs_5_.1, ...), custom_call_target="tpu_custom_call" | custom-call | tf_op jit(solution)/shard_map/pallas_call | solution.py:1664
  125.0 4.1 %shard_map.87 = (f32[1,213504]{1,0:T(1,128)}, bf16[8000,256]{1,0:T(8,128)(2,1)}) custom-call(f32[1680,128]{1,0:T(8,128)} %get-tuple-element.4.weight_rows, bf16[8000,256]{1,0:T(8,128)(2,1)} %get-tuple-element.5.input_rows), custom_call_target="tpu_custom_call" | custom-call | tf_op jit(solution)/shard_map/pallas_call | solution.py:1674

commit v5 on v3

--- a/solution.py
+++ b/solution.py
@@ -22,7 +22,7 @@
 SOFTMAX_TEMPER = 0.07
 EPSILON = 1e-05
 
-PAD = 48
+PAD = 40
 ROW = GRAD_LEN // LANES
 ROWS = -(-ROW // 16) * 16
 BLOCK = 16
@@ -45,6 +45,7 @@
 SPANS = {2: 16, 5: 8, 6: 8, 9: 16}
 STARTS = {2: 0, 5: 16, 6: 24, 9: 32}
 SPAN_ROWS = 48
+NARROW = [number for number in range(EXCHANGES) if number not in SPANS]
 
 PIECES = ((3, 1032), (2, 1668), (1, 1552), (0, 9 * MID), (0, 260))
 LAST, THIRD, SECOND, FIRST_MID, FIRST_IN = range(5)
@@ -299,12 +300,12 @@
     def outgoing(number):
         if number in SPANS:
             return k.send.at[pl.ds(STARTS[number], SPANS[number])]
-        return k.send_narrow.at[number]
+        return k.send_narrow.at[NARROW.index(number)]
 
     def incoming(number, which):
         if number in SPANS:
             return k.recv.at[which, pl.ds(STARTS[number], SPANS[number])]
-        return k.recv_narrow.at[number, which]
+        return k.recv_narrow.at[NARROW.index(number), which]
 
     def share(number):
         def give(i, carry):
@@ -490,7 +491,7 @@
         give_scatter(number)
 
     def put_narrow(number, row, vector):
-        k.send_narrow[number, row : row + 1, :] = vector
+        k.send_narrow[NARROW.index(number), row : row + 1, :] = vector
 
     def put_wide(number, row, vectors):
         for j, vector in enumerate(vectors):
@@ -653,6 +654,9 @@
 
     def turned(piece):
         return piece.astype(BF16).T
+
+    def turned_rows(ref, lane=0):
+        return turned(ref[:, lane * LANES : (lane + 1) * LANES])
 
     to_rows(EARLY, ROW)
     weight_copies = weight_copies + send_weights(1)
@@ -742,7 +746,7 @@
         k.turn[0:LANES, :] = turned(jnp.where(live, t1[rows, :], 0.0))
         live = lax.broadcasted_iota(jnp.int32, (16, out_rows), 1) + block * out_rows < 4 * rows_live
         k.turn[LANES : LANES + 16, :] = jnp.where(live, 1.0, 0.0).astype(BF16)
-        found = dense(k.turn[...], feat[rows, :])
+        found = dense(k.turn[0 : LANES + 16, :], feat[rows, :])
         for half in range(2):
             at = slice(half * LANES, (half + 1) * LANES)
             product = found[0:LANES, lanes(half)].T
@@ -916,6 +920,11 @@
     unpack_wide(0, MID, k.wout4)
     bank_to_bf16(1)
     keep_second_slope()
+    ones = jnp.ones((out_rows, LANES), BF16)
+    for half in range(2):
+        k.turn[half * LANES : (half + 1) * LANES, :] = turned_rows(k.xs, half)
+    k.gram_s[...] = dense(k.turn[0:CIN, :], k.xs[...])
+    k.sum_s[...] = dense(k.turn[0:CIN, :], ones)
     collect(3)
     finish(L4, narrow(0), narrow(1), gain_narrow(4), gain_narrow(5), inverse_count)
 
@@ -964,6 +973,9 @@
         )
         gn[pl.ds(slot, LANES, stride=8), :] = found
     first_products(2)
+    k.turn[0:MID, :] = turned_rows(k.h2)
+    k.gram2[...] = dense(k.turn[0:MID, :], k.h2[...])
+    k.sum2[...] = dense(k.turn[0:MID, :], ones)
     collect(4)
     finish(L5, narrow(0), narrow(1), gain_narrow(6), gain_narrow(7), inverse_count)
     close_narrow(L5, k.t5, k.h4)
@@ -1168,9 +1180,6 @@
                     r * LANES : (r + 1) * LANES, lanes(j)
                 ]
 
-    def turned_rows(ref, lane=0):
-        return turned(ref[:, lane * LANES : (lane + 1) * LANES])
-
     k.turn[0:LANES, :] = turned_rows(k.h4)
     put_wide_matrix(0, dense(k.turn[0:LANES, :], wide2[0:out_rows, :]))
     stage_piece(LAST)
@@ -1262,8 +1271,17 @@
     wst[THIRD_GAIN : THIRD_BIAS + 1, :] = k.small[0:2, :]
     wst[THIRD_MID_GAIN : THIRD_MID_BIAS + 1, :] = k.small[2:4, :]
     stage_piece(THIRD)
+    k.turn[0:MID, :] = turned_rows(k.h2)
+    for half in range(2):
+        k.turn[MID + half * LANES : MID + (half + 1) * LANES, :] = turned_rows(k.xs, half)
+    for pair in range(2):
+        found = dense(k.turn[0 : MID + CIN, :], gw[:, 2 * pair * LANES : 2 * (pair + 1) * LANES])
+        for r, at in enumerate((0, AFTER_OUT, AFTER_OUT + 4 * LANES)):
+            for j in range(2):
+                wst[pl.ds(at + 2 * pair + j, LANES, stride=4), :] = found[
+                    r * LANES : (r + 1) * LANES, lanes(j)
+                ]
     give_home(LAST)
-    keep_first_slope()
     collect(9)
     finish_back(L3, wide(0), wide(1), gain_wide(8), inverse_count)
     finish_back(LS, wide(0), wide(2), gain_wide(16), inverse_count)
@@ -1288,13 +1306,23 @@
         wst[OUT_BIAS + j : OUT_BIAS + j + 1, :] = bias_grads[j]
         wst[SHORT_GAIN + j : SHORT_GAIN + j + 1, :] = short_grads[j]
         wst[SHORT_BIAS + j : SHORT_BIAS + j + 1, :] = bias_grads[j]
-    k.turn[0:LANES, :] = turned_rows(k.h2)
-    put_wide_matrix(0, dense(k.turn[0:LANES, :], wide2[0:out_rows, :]))
+
+    def by_linearity(at, layer, products, sums):
+        for j in range(4):
+            rows = pl.ds(at + j, LANES, stride=4)
+            wst[rows, :] = (
+                wst[rows, :] * get_coef(layer, GRAD_A, j)
+                - products[:, lanes(j)] * get_coef(layer, GRAD_E, j)
+                - sums * get_coef(layer, GRAD_D, j)
+            )
+
+    high, low = split(k.gram2[...])
+    by_linearity(0, L3, dense(high, k.wout2[...]) + dense(low, k.wout2[...]), k.sum2[...])
+    high, low = split(k.gram_s[...])
+    products = dense(high, k.wshort[...]) + dense(low, k.wshort[...])
     for half in range(2):
-        k.turn[0:LANES, :] = turned_rows(k.xs, half)
-        put_wide_matrix(
-            AFTER_OUT + half * 4 * LANES, dense(k.turn[0:LANES, :], wide2[out_rows : 2 * out_rows, :])
-        )
+        rows = slice(half * LANES, (half + 1) * LANES)
+        by_linearity(AFTER_OUT + half * 4 * LANES, LS, products[rows, :], k.sum_s[rows, :])
     stage_piece(SECOND)
     give_line(THIRD)
 
@@ -1308,6 +1336,7 @@
     each_chunk(back_picked)
     for half in range(2):
         big2[half * plane : half * plane + PAD, :] = jnp.zeros((PAD, LANES), F32)
+    keep_first_slope()
     collect(10)
     finish_back(L2, narrow(0), narrow(1), gain_narrow(2), inverse_count)
     back_close(L2, k.t2)
@@ -1604,7 +1633,11 @@
         "gw": low(out_rows, COUT),
         "wide2": low(BANK // 4, COUT),
         "dtn": low(out_rows, MID),
-        "turn": low(LANES + 16, out_rows),
+        "turn": low(MID + CIN, out_rows),
+        "gram2": held(MID, MID),
+        "gram_s": held(CIN, CIN),
+        "sum2": held(MID, LANES),
+        "sum_s": held(CIN, LANES),
         "first_t": held(CIN, MID),
         "first_s": held(CIN, MID),
         "masks": low(4, out_rows, LANES),
@@ -1632,8 +1665,8 @@
         "tabv": held(16, TABLE, dtype=jnp.int32),
         "tab": pltpu.SMEM((16, TABLE), jnp.int32),
         "send": held(SPAN_ROWS, LANES),
-        "send_narrow": held(EXCHANGES, 2, LANES),
-        "recv_narrow": held(EXCHANGES, batches, 2, LANES),
+        "send_narrow": held(len(NARROW), 2, LANES),
+        "recv_narrow": held(len(NARROW), batches, 2, LANES),
         "recv": held(batches, SPAN_ROWS, LANES),
         "total": held(16, LANES),
         "gb": low(sum(padded), LANES),

time: 125 us -> 125 us (level)
  no operation moved by 1% of the time
where the time goes in v5:
time: 125 us
  Pallas kernels  123 us (98%)
  between operations  1.47 us (1%)
    pallas_call x1, Pallas kernels, shards(): pl.pallas_call(functools.partial(kernel, names, batches, phases, in_rows,...  119 us
    pallas_call x1, Pallas kernels, shards(): pl.pallas_call(write_kernel, out_shape=(jax.ShapeDtypeStruct((1, GRAD_LEN...  4.1 us

profile of v5, /device:TPU:0, one launch (start us, length us, event | category | flops | bytes accessed | tf_op | source)
XLA Modules:
  0.0 124.6 jit_solution(9244180053862137508)
XLA Ops:
  1.3 119.1 %shard_map.86 = (f32[1680,128]{1,0:T(8,128)}, bf16[8000,256]{1,0:T(8,128)(2,1)}) custom-call(bf16[32000,256]{1,0:T(8,128)(2,1)} %refs_0_.1, bf16[1,213504]{1,0:T(2,128)(2,1)} %refs_1_.1, s32[1,5,4,4096]{3,2,1,0:T(4,128)} %bitcast.2, f32[16384,128]{1,0:T(8,128)} %refs_3_.1, s32[5,4,8]{2,1,0:T(4,128)} %bitcast.3, s32[1,4,5]{2,1,0:T(4,128)} %refs_5_.1, ...), custom_call_target="tpu_custom_call" | custom-call | tf_op jit(solution)/shard_map/pallas_call | solution.py:1697
  120.4 4.1 %shard_map.87 = (f32[1,213504]{1,0:T(1,128)}, bf16[8000,256]{1,0:T(8,128)(2,1)}) custom-call(f32[1680,128]{1,0:T(8,128)} %get-tuple-element.4.weight_rows, bf16[8000,256]{1,0:T(8,128)(2,1)} %get-tuple-element.5.input_rows), custom_call_target="tpu_custom_call" | custom-call | tf_op jit(solution)/shard_map/pallas_call | solution.py:1707
